TPU v7x, 256 devices: a whole 4x4x8 slice. The times are simulated.
256 devices in a mesh: sim: 32 (over z, y_lo, core), pen: 8 (over y_hi, x).
Axes of the slice: x: 4, y: 4 (y_hi: 2, y_lo: 2; y = y_hi * 2 + y_lo), z: 8, core: 2. Of those that a mesh axis runs over, the one named last changes fastest.
Arguments:
- density: float32 [1024, 32, 1024], P('sim', None, 'pen'), may hold values from 0.05 to 2
- velocity: float32 [3, 1024, 32, 1024], P(None, 'sim', None, 'pen'), may hold values from -4 to 4
- stencil_code: int32 [1024, 32, 1024], P('sim', None, 'pen'), may hold values from 0 to 7
- fractions: float32 [3, 1024, 32, 1024], P(None, 'sim', None, 'pen'), may hold values from 0 to 1
- targets: float32 [32, 32, 1024], P(None, 'sim', 'pen'), may hold values from 0.2 to 1.2
- view_start: int32 [32], replicated, may hold values from 0 to 1023
- view_sign: int32 [32], replicated, may hold values from 0 to 1
Outputs:
- density_new: float32 [1024, 32, 1024], P('sim', None, 'pen')
- velocity_new: float32 [3, 1024, 32, 1024], P(None, 'sim', None, 'pen')
- images: float32 [32, 32, 1024], P(None, 'sim', 'pen')
- density_grad: float32 [1024, 32, 1024], P('sim', None, 'pen')
Inputs may be any that keep to these rules, and one draw needn't show every extreme that they name: `stencil_code`: bits 0, 1 and 2 of an entry belong to the first, second and third grid dimension.
All inputs are finite; a program needn't handle non-finite values.
Results may differ from a plain program's by a relative error of at most 0.0003.
Values sent between devices are 32-bit elements; how exact they have to be, the bound alone decides.
A program may use at most 192 MiB of HBM per device.

v0:
```python
import math

import jax
import jax.numpy as jnp
from jax import lax
from jax.sharding import PartitionSpec as P

STEPS = 256


shift_values = (-1, 0, 1)
einsum_forms = {1: "kx,rxzy->rkzy", 3: "ky,rxzy->rxzk"}


def extended(cells, sides, width):
    for axis, dim in sides:
        count = lax.axis_size(axis)
        head = lax.slice_in_dim(cells, 0, width, axis=dim)
        tail = lax.slice_in_dim(cells, cells.shape[dim] - width, cells.shape[dim], axis=dim)
        cells = jnp.concatenate(
            [
                lax.ppermute(tail, axis, [(i, (i + 1) % count) for i in range(count)]),
                cells,
                lax.ppermute(head, axis, [((i + 1) % count, i) for i in range(count)]),
            ],
            axis=dim,
        )
    return cells


def stencil_weights(offset_bit, fraction):
    lower_weight = jnp.where(offset_bit == 1, 1.0 - fraction, 0.0)
    center_weight = jnp.where(offset_bit == 1, fraction, 1.0 - fraction)
    upper_weight = jnp.where(offset_bit == 1, 0.0, fraction)
    return (lower_weight, center_weight, upper_weight)


def with_rim(fields):
    return extended(fields, (("sim", 1), ("pen", 3)), 1)


def dft_tables(length):
    row_index = lax.broadcasted_iota(jnp.int32, (length, length), 0)
    col_index = lax.broadcasted_iota(jnp.int32, (length, length), 1)
    angles = (row_index * col_index % length).astype(jnp.float32) * (2.0 * math.pi / length)
    return (jnp.cos(angles), jnp.sin(angles))


def transform_axis(table, spectrum, which_axis):
    return jnp.einsum(
        einsum_forms[which_axis],
        table,
        spectrum,
        precision=lax.Precision.HIGHEST,
        preferred_element_type=jnp.float32,
    )


def forward_real(table_set, values, which_axis):
    cos_part = transform_axis(table_set[0], values, which_axis)
    sin_part = transform_axis(table_set[1], values, which_axis)
    return jnp.concatenate([cos_part, -sin_part], axis=0)


def forward_step(table_set, spectrum, which_axis):
    cos_part = transform_axis(table_set[0], spectrum, which_axis)
    sin_part = transform_axis(table_set[1], spectrum, which_axis)
    return jnp.stack([cos_part[0] + sin_part[1], cos_part[1] - sin_part[0]])


def inverse_step(table_set, spectrum, which_axis, length):
    cos_part = transform_axis(table_set[0], spectrum, which_axis)
    sin_part = transform_axis(table_set[1], spectrum, which_axis)
    return jnp.stack([(cos_part[0] - sin_part[1]) / length, (cos_part[1] + sin_part[0]) / length])


def inverse_real(table_set, spectrum, which_axis, length):
    cos_part = transform_axis(table_set[0], spectrum, which_axis)
    sin_part = transform_axis(table_set[1], spectrum, which_axis)
    return (cos_part[0] - sin_part[1]) / length


def eigenvalue_of(frequency, length):
    phases = frequency.astype(jnp.float32) * (math.pi / length)
    sines = jnp.sin(phases)
    return 4.0 * sines * sines


def render(ray_density, targets, view_start, view_sign):
    grid_x = ray_density.shape[1]
    pixels = ray_density.shape[2] * ray_density.shape[3]
    view_count = targets.shape[0]
    absorb = 2.0 / STEPS
    flat_density = ray_density.reshape(grid_x, pixels)
    offsets = lax.broadcasted_iota(jnp.int32, (1, STEPS), 1)
    cell_index = (view_start[:, None] + (2 * view_sign[:, None] - 1) * offsets) % grid_x
    samples = jnp.take(flat_density, cell_index, axis=0)
    row_index = lax.broadcasted_iota(jnp.int32, (STEPS, STEPS), 0)
    col_index = lax.broadcasted_iota(jnp.int32, (STEPS, STEPS), 1)
    ordered = (row_index > col_index).astype(jnp.float32)
    optical_depth = absorb * jnp.einsum(
        "st,vtq->vsq",
        ordered,
        samples,
        precision=lax.Precision.HIGHEST,
        preferred_element_type=jnp.float32,
    )
    transmit = jnp.exp(-optical_depth)
    emitted = absorb * samples * transmit
    images = jnp.sum(emitted, axis=1)
    later_light = jnp.einsum(
        "ts,vtq->vsq",
        ordered,
        emitted,
        precision=lax.Precision.HIGHEST,
        preferred_element_type=jnp.float32,
    )
    residual = images - targets.reshape(view_count, pixels)
    grad_terms = STEPS * residual[:, None, :] * (absorb * transmit - absorb * later_light)
    gradient = (
        jnp.zeros((grid_x, pixels), jnp.float32)
        .at[cell_index.reshape(-1)]
        .add(grad_terms.reshape(-1, pixels))
    )
    return (images.reshape(targets.shape), gradient.reshape(ray_density.shape[1:]))


def shards(density, velocity, stencil_code, fractions, targets, view_start, view_sign):
    local_x, layers, local_y = density.shape
    sim_count = lax.axis_size("sim")
    pen_count = lax.axis_size("pen")
    grid_x = local_x * sim_count
    grid_y = local_y * pen_count
    weight_x = stencil_weights(stencil_code % 2, fractions[0])
    weight_z = stencil_weights(stencil_code // 2 % 2, fractions[1])
    weight_y = stencil_weights(stencil_code // 4 % 2, fractions[2])
    fields = jnp.concatenate([density[None], velocity], axis=0)
    widened = with_rim(fields)
    summed = jnp.zeros_like(fields)
    for slot_x, shift_x in enumerate(shift_values):
        for slot_y, shift_y in enumerate(shift_values):
            shifted = widened[
                :, 1 + shift_x : 1 + shift_x + local_x, :, 1 + shift_y : 1 + shift_y + local_y
            ]
            z_summed = jnp.zeros_like(fields)
            for slot_z, shift_z in enumerate(shift_values):
                z_summed = z_summed + weight_z[slot_z] * jnp.roll(shifted, -shift_z, axis=2)
            summed = summed + weight_x[slot_x] * weight_y[slot_y] * z_summed
    density_new = summed[0]
    moved_x = summed[1]
    moved_z = summed[2]
    moved_y = summed[3]
    rimmed = with_rim(jnp.stack([moved_x, moved_y]))
    divergence = (
        moved_x
        - rimmed[0, 0:local_x, :, 1 : 1 + local_y]
        + (moved_y - rimmed[1, 1 : 1 + local_x, :, 0:local_y])
    )
    tables_x = dft_tables(grid_x)
    in_rays = (
        lax.all_to_all(density_new[None], "sim", split_axis=2, concat_axis=1, tiled=True),
        lax.all_to_all(divergence[None], "sim", split_axis=2, concat_axis=1, tiled=True),
    )
    ray_density, spread_div = in_rays
    spectrum = forward_real(tables_x, spread_div, 1)
    spectrum = lax.all_to_all(spectrum, "pen", split_axis=1, concat_axis=3, tiled=True)
    spectrum = forward_step(tables_x, spectrum, 3)
    block_x = grid_x // pen_count
    freq_x = lax.axis_index("pen") * block_x + lax.broadcasted_iota(jnp.int32, (block_x, 1, 1), 0)
    freq_y = lax.broadcasted_iota(jnp.int32, (1, 1, grid_y), 2)
    eigenvalue = eigenvalue_of(freq_x, grid_x) + eigenvalue_of(freq_y, grid_y)
    at_anchor = (freq_x == 0) & (freq_y == 0)
    solved = jnp.where(at_anchor, 0.0, spectrum / jnp.where(at_anchor, 1.0, -eigenvalue))
    spectrum = inverse_step(tables_x, solved, 3, grid_y)
    spectrum = lax.all_to_all(spectrum, "pen", split_axis=3, concat_axis=1, tiled=True)
    ray_pressure = inverse_real(tables_x, spectrum, 1, grid_x)
    images, gradient = render(ray_density, targets, view_start, view_sign)
    returned = (
        lax.all_to_all(ray_pressure[None], "sim", split_axis=1, concat_axis=2, tiled=True),
        lax.all_to_all(gradient[None], "sim", split_axis=1, concat_axis=2, tiled=True),
    )
    pressure_block, density_grad = returned
    pressure = pressure_block[0]
    padded = with_rim(pressure[None])
    velocity_new = jnp.stack(
        [
            moved_x - (padded[0, 2 : 2 + local_x, :, 1 : 1 + local_y] - pressure),
            moved_z,
            moved_y - (padded[0, 1 : 1 + local_x, :, 2 : 2 + local_y] - pressure),
        ]
    )
    return (density_new, velocity_new, images, density_grad[0])


def solution(mesh):
    placed = (
        P("sim", None, "pen"),
        P(None, "sim", None, "pen"),
        P("sim", None, "pen"),
        P(None, "sim", None, "pen"),
        P(None, "sim", "pen"),
        P(),
        P(),
    )
    return jax.shard_map(
        shards,
        mesh=mesh,
        in_specs=placed,
        out_specs=(
            P("sim", None, "pen"),
            P(None, "sim", None, "pen"),
            P(None, "sim", "pen"),
            P("sim", None, "pen"),
        ),
        check_vma=False,
    )
```

profile of v0, /device:TPU:1, one launch (start us, length us, event | category | flops | bytes accessed | tf_op | source)
XLA Modules:
  0.0 531.8 jit_solution(13535654448050438118)
XLA Ops:
  0.6 2.4 copy.40
  3.4 2.8 collective-permute-start
  6.9 2.6 fusion.108
  9.5 1.3 subtract_select_fusion.1
  12.0 1.1 copy.49
  13.1 1.1 copy.50
  14.3 1.1 copy.51
  15.4 1.1 copy.52
  16.5 1.1 copy.53
  17.6 1.1 copy.54
  18.8 1.1 copy.43
  19.9 1.1 copy.44
  21.1 1.1 copy.37
  22.2 1.1 copy.38
  23.7 3.1 fusion.214
  26.8 2.7 copy.41
  30.5 3.3 copy.47
  33.9 4.5 collective-permute-start.3
  38.9 4.1 fusion.212
  43.7 2.6 copy.42
  46.3 3.3 copy.48
  49.7 6.6 %maximum_maximum_fusion = (f32[4,34,32,129]{3,1,2,0:T(8,128)}, f32[4,34,32,129]{3,1,2,0:T(8,128)S(1)}) fusion(f32[4,1,32,128]{3,1,2,0:T(1,128)S(1)} %collective-permute-done.1, f32[3,32,32,128]{3,1,2,0:T(8,128)S(1)} %copy.40, f32[1,32,32,128]{3,1,2,0:T(8,128)S(1)} %bitcast.176, f32[4,1,32,128]{3,1,2,0:T(1,128)S(1)} %collective-permute-done, ...), kind=kLoop, calls=%fused_computation.12 | loop fusion | flops 4491264 | bytes 6754304 | tf_op jit(solution)/shard_map/concatenate | solution.py:20
  56.3 6.1 %fusion.210 = (f32[4,32,31,128]{3,1,2,0:T(8,128)}, f32[4,32,31,128]{3,1,2,0:T(8,128)}, f32[4,32,31,128]{3,1,2,0:T(8,128)}, f32[4,32,31,128]{3,1,2,0:T(8,128)}, f...) fusion(f32[4,34,32,129]{3,1,2,0:T(8,128)S(1)} %get-tuple-element.38), kind=kLoop, calls=%fused_computation.357 | loop fusion | bytes 24379392 | tf_op jit(solution)/shard_map/jit(_roll_static)/slice | solution.py:147
  62.4 10.9 %fusion.211 = (f32[4,32,31,128]{3,1,2,0:T(8,128)}, f32[4,32,31,128]{3,1,2,0:T(8,128)}, f32[4,32,31,128]{3,1,2,0:T(8,128)}, f32[4,32,31,128]{3,1,2,0:T(8,128)}, f...) fusion(f32[4,34,32,129]{3,1,2,0:T(8,128)} %get-tuple-element.37), kind=kLoop, calls=%fused_computation.358 | loop fusion | bytes 24379392 | tf_op jit(solution)/shard_map/jit(_roll_static)/slice | solution.py:147
  73.3 30.8 %fusion.29 = f32[4,32,32,128]{3,1,2,0:T(8,128)S(1)} fusion(f32[3,32,32,128]{3,1,2,0:T(8,128)S(1)} %copy.40, f32[1,32,32,128]{3,1,2,0:T(8,128)S(1)} %bitcast.177, f32[4,34,32,1]{3,1,2,0:T(8,128)} %copy.48, f32[4,1,32,128]{3,1,2,0:T(1,128)S(1)} %collective-permute-done.1, f32[4,1,32,128]{3,1,2,0:T(1,128)S(1)} %collective-permute-done, ...), kind=kLoop, calls=%fused_computation.56 | loop fusion | flops 71827456 | bytes 64129024 | tf_op jit(solution)/shard_map/add | solution.py:148
  104.1 1.3 copy-done.3
  105.5 1.7 collective-permute-start.4
  107.3 3.6 collective-permute-start.5
  112.9 6.4 %collective-permute-done.6 = f32[2,34,32,1]{1,2,3,0:T(8,128)S(1)} collective-permute-done((f32[2,34,32,1]{1,2,3,0:T(8,128)S(1)}, f32[2,34,32,1]{1,2,3,0:T(8,128)S(1)}, u32[]{:S(2)}, u32[]{:S(2)}) %collective-permute-start.6) | collective-permute-done | bytes 8736 | tf_op jit(solution)/shard_map/ppermute | solution.py:22
  120.1 28.4 %all_to_all.93 = f32[1,32,32,128]{3,1,0,2:T(8,128)S(1)} all-to-all(f32[1,32,32,128]{3,1,0,2:T(8,128)S(1)} %fusion.142), channel_id=1, replica_groups=mesh['sim'=32,'pen'=8] {'sim'}, dimensions={2} | all-to-all | bytes 1048576 | tf_op jit(solution)/shard_map/all_to_all | solution.py:162
  148.5 19.9 %fusion.115 = f32[1,1024,1,128]{1,3,2,0:T(8,128)S(1)} fusion(f32[1024,128]{1,0:T(8,128)S(1)} %bitcast.188), kind=kOutput, calls=%fused_computation.200 | convolution fusion | flops 1625292800 | bytes 1048576 | tf_op jit(solution)/shard_map/kx,rxzy->rkzy/dot_general | solution.py:50
  168.4 20.0 %fusion.121 = f32[1,1024,1,128]{1,3,2,0:T(8,128)S(1)} fusion(f32[1024,128]{1,0:T(8,128)S(1)} %bitcast.189), kind=kOutput, calls=%fused_computation.202 | convolution fusion | flops 1625423872 | bytes 1048576 | tf_op jit(solution)/shard_map/kx,rxzy->rkzy/dot_general | solution.py:50
  188.5 1.9 copy.58
  190.4 4.6 all-to-all-start.1
  195.4 16.9 %all-to-all-done.1 = f32[2,1024,1,128]{3,2,0,1:T(1,128)S(1)} async-done(((f32[2,1024,1,128]{3,2,0,1:T(1,128)}), f32[2,1024,1,128]{3,2,0,1:T(1,128)S(1)}, u32[]{:S(2)}, u32[]{:S(2)}) %all-to-all-start.1) | async-done | bytes 1048608 | tf_op jit(solution)/shard_map/all_to_all | solution.py:166
  213.1 20.0 %fusion.14 = f32[2,128,1024]{2,1,0:T(8,128)S(1)} fusion(f32[2,128,1024]{2,1,0:T(8,128)S(1)} %reshape.497), kind=kOutput, calls=%fused_computation.31 | convolution fusion | flops 3235905536 | bytes 2097152 | tf_op jit(solution)/shard_map/ky,rxzy->rxzk/dot_general | solution.py:50
  233.0 20.5 %fusion.8 = f32[2,128,1024]{2,1,0:T(8,128)S(1)} fusion(f32[2,128,1024]{2,1,0:T(8,128)S(1)} %reshape.497), kind=kOutput, calls=%fused_computation.25 | convolution fusion | flops 3235905536 | bytes 2097152 | tf_op jit(solution)/shard_map/ky,rxzy->rxzk/dot_general | solution.py:50
  253.7 19.2 %fusion.12 = f32[2,128,1024]{2,1,0:T(8,128)S(1)} fusion(f32[1,128,1024]{2,1,0:T(8,128)S(1)} %get-tuple-element.45, f32[1,128,1024]{2,1,0:T(8,128)S(1)} %get-tuple-element.44, f32[128,1024]{1,0:T(8,128)S(1)} %negate_select_fusion.11, pred[128,1024]{1,0:T(8,128)(4,1)S(1)} %broadcast_and_fusion), kind=kOutput, calls=%fused_computation.29 | convolution fusion | flops 3236691968 | bytes 2752512 | tf_op jit(solution)/shard_map/ky,rxzy->rxzk/dot_general | solution.py:50
  273.0 19.6 %fusion.6 = f32[2,128,1024]{2,1,0:T(8,128)S(1)} fusion(f32[1,128,1024]{2,1,0:T(8,128)S(1)} %get-tuple-element.45, f32[1,128,1024]{2,1,0:T(8,128)S(1)} %get-tuple-element.44, f32[128,1024]{1,0:T(8,128)S(1)} %negate_select_fusion.11, pred[128,1024]{1,0:T(8,128)(4,1)S(1)} %broadcast_and_fusion), kind=kOutput, calls=%fused_computation.23 | convolution fusion | flops 3236691968 | bytes 2752512 | tf_op jit(solution)/shard_map/ky,rxzy->rxzk/dot_general | solution.py:50
  293.6 19.0 %all_to_all.94 = f32[2,128,1,1024]{1,2,0,3:T(1,128)S(1)} all-to-all(f32[2,128,1,1024]{1,2,0,3:T(1,128)S(1)} %copy.60), channel_id=1, replica_groups=mesh['sim'=32,'pen'=8] {'pen'}, dimensions={3} | all-to-all | bytes 2097152 | tf_op jit(solution)/shard_map/all_to_all | solution.py:175
  313.4 20.0 %fusion.109 = f32[2,1024,1,128]{1,3,0,2:T(8,128)S(1)} fusion(f32[2,1024,128]{1,2,0:T(8,128)S(1)} %reshape.498), kind=kOutput, calls=%fused_computation.195 | convolution fusion | flops 3235905536 | bytes 2097152 | tf_op jit(solution)/shard_map/kx,rxzy->rkzy/dot_general | solution.py:50
  333.4 20.1 %fusion.112 = f32[2,1024,1,128]{1,3,0,2:T(8,128)S(1)} fusion(f32[2,1024,128]{1,2,0:T(8,128)S(1)} %reshape.498), kind=kOutput, calls=%fused_computation.196 | convolution fusion | flops 3235905536 | bytes 2097152 | tf_op jit(solution)/shard_map/kx,rxzy->rkzy/dot_general | solution.py:50
  353.6 1.0 copy.62
  354.6 5.8 %all-to-all-start.3 = ((f32[1,1024,1,128]{3,0,2,1:T(1,128)}), f32[1,1024,1,128]{3,0,2,1:T(1,128)S(1)}, u32[]{:S(2)}, u32[]{:S(2)}) async-start(f32[1,1024,1,128]{3,0,2,1:T(1,128)} %copy.62), calls=%async_computation.3 | async-start | bytes 1048576 | tf_op jit(solution)/shard_map/all_to_all | solution.py:179
  360.5 16.5 %all-to-all-done.3 = f32[1,1024,1,128]{3,0,2,1:T(1,128)S(1)} async-done(((f32[1,1024,1,128]{3,0,2,1:T(1,128)}), f32[1,1024,1,128]{3,0,2,1:T(1,128)S(1)}, u32[]{:S(2)}, u32[]{:S(2)}) %all-to-all-start.3) | async-done | bytes 524320 | tf_op jit(solution)/shard_map/all_to_all | solution.py:179
  377.1 1.8 collective-permute-start.7
  379.0 1.2 collective-permute-start.8
  380.2 1.3 collective-permute-done.7
  381.9 1.3 collective-permute-start.9
  383.3 1.2 collective-permute-done.9
  384.9 1.8 fusion.134
  386.7 8.8 %all-to-all-start.4 = ((f32[1,32,32,128]{3,1,0,2:T(8,128)}), f32[1,32,32,128]{3,1,0,2:T(8,128)S(1)}, u32[]{:S(2)}, u32[]{:S(2)}) async-start(f32[1,32,32,128]{3,1,0,2:T(8,128)} %get-tuple-element.39), calls=%async_computation.4 | async-start | bytes 1048576 | tf_op jit(solution)/shard_map/all_to_all | solution.py:161
  395.6 16.6 %all-to-all-done.4 = f32[1,32,32,128]{3,1,0,2:T(8,128)S(1)} async-done(((f32[1,32,32,128]{3,1,0,2:T(8,128)}), f32[1,32,32,128]{3,1,0,2:T(8,128)S(1)}, u32[]{:S(2)}, u32[]{:S(2)}) %all-to-all-start.4) | async-done | bytes 524320 | tf_op jit(solution)/shard_map/all_to_all | solution.py:161
  412.2 27.8 %gather_fusion = f32[8192,128]{1,0:T(8,128)} fusion(f32[1024,128]{1,0:T(8,128)S(1)} %bitcast.170, s32[8192]{0:T(1024)S(1)} %broadcast_clamp_fusion), kind=kCustom, calls=%fused_computation | custom fusion | bytes 8421376 | tf_op jit(solution)/shard_map/jit(_take)/gather | solution.py:97
  440.0 5.7 %copy.66 = f32[32,256,128]{1,2,0:T(8,128)} copy(f32[32,256,128]{2,1,0:T(8,128)} %bitcast.178) | data formatting | bytes 8388608 | tf_op jit(solution)/shard_map/jit(_take)/gather | solution.py:97
  445.7 6.6 %fusion.89 = (f32[32,128]{1,0:T(8,128)S(1)}, f32[32,128,256]{2,1,0:T(8,128)S(1)}) fusion(f32[32,256,128]{1,2,0:T(8,128)} %copy.66, pred[32,256]{1,0:T(8,128)(4,1)S(1)} %compare_and_fusion), kind=kOutput, calls=%fused_computation.182 | convolution fusion | flops 3228626944 | bytes 8413184 | tf_op jit(solution)/shard_map/st,vtq->vsq/dot_general | solution.py:101
  452.3 5.0 fusion.3
  457.3 5.7 %copy.67 = f32[32,256,128]{2,1,0:T(8,128)} copy(f32[32,256,128]{1,2,0:T(8,128)} %fusion.3) | data formatting | bytes 8388608 | tf_op jit(solution)/shard_map/mul | solution.py:119
  463.0 45.1 %scatter_custom_fusion = f32[1024,128]{1,0:T(8,128)} fusion(s32[8192]{0:T(1024)S(1)} %bitcast.192, f32[8192,128]{1,0:T(8,128)} %bitcast.182, f32[]{:T(128)} %constant.109.clone.1), kind=kCustom, calls=%fused_computation.280 | custom fusion | flops 1048576 | bytes 524800 | tf_op jit(solution)/shard_map/scatter-add | solution.py:123
  508.1 5.1 all-to-all-start.5
  513.4 2.1 copy.69
  515.4 1.1 copy.68
  516.5 13.7 %all-to-all-done.5 = f32[1,1024,1,128]{3,2,0,1:T(1,128)S(1)} async-done(((f32[1,1024,1,128]{3,2,0,1:T(1,128)}), f32[1,1024,1,128]{3,2,0,1:T(1,128)S(1)}, u32[]{:S(2)}, u32[]{:S(2)}) %all-to-all-start.5) | async-done | bytes 524320 | tf_op jit(solution)/shard_map/all_to_all | solution.py:180
  530.3 1.1 copy.70
  (88 shorter events, 12.6 us)
Async XLA Ops:
  0.6 2.4 copy-start.12
  3.4 19.9 %collective-permute-start = (f32[4,1,32,128]{3,1,2,0:T(1,128)S(1)}, f32[4,1,32,128]{3,1,2,0:T(1,128)S(1)}, u32[]{:S(2)}, u32[]{:S(2)}) collective-permute-start(f32[4,1,32,128]{3,1,2,0:T(1,128)S(1)} %get-tuple-element.57), channel_id=1, source_target_pairs={{0,8},{8,16},{16,24},{24,32},{32,40},{40,48},{48,56},{56,64},{64,7... | collective-permute-start | bytes 196616 | tf_op jit(solution)/shard_map/ppermute | solution.py:22
  6.2 3.3 copy-start.5
  6.2 3.3 copy-start.11
  6.2 17.1 %collective-permute-start.1 = (f32[4,1,32,128]{3,1,2,0:T(1,128)S(1)}, f32[4,1,32,128]{3,1,2,0:T(1,128)S(1)}, u32[]{:S(2)}, u32[]{:S(2)}) collective-permute-start(f32[4,1,32,128]{3,1,2,0:T(1,128)S(1)} %get-tuple-element.58), channel_id=1, source_target_pairs={{8,0},{16,8},{24,16},{32,24},{40,32},{48,40},{56,48},{64,56},{72,6... | collective-permute-start | bytes 196616 | tf_op jit(solution)/shard_map/ppermute | solution.py:24
  29.6 14.1 %collective-permute-start.2 = (f32[4,34,32,1]{1,2,3,0:T(8,128)S(1)}, f32[4,34,32,1]{1,2,3,0:T(8,128)S(1)}, u32[]{:S(2)}, u32[]{:S(2)}) collective-permute-start(f32[4,34,32,1]{1,2,3,0:T(8,128)S(1)} %copy.41), channel_id=1, source_target_pairs={{0,1},{1,2},{2,3},{3,4},{4,5},{5,6},{6,7},{7,0},{8,9},{9,10},{10,1... | collective-permute-start | bytes 52232 | tf_op jit(solution)/shard_map/ppermute | solution.py:22
  33.9 12.5 %collective-permute-start.3 = (f32[4,34,32,1]{1,2,3,0:T(8,128)}, f32[4,34,32,1]{1,2,3,0:T(8,128)}, u32[]{:S(2)}, u32[]{:S(2)}) collective-permute-start(f32[4,34,32,1]{1,2,3,0:T(8,128)} %copy.47), channel_id=1, source_target_pairs={{1,0},{2,1},{3,2},{4,3},{5,4},{6,5},{7,6},{0,7},{9,8},{10,9},{11,1... | collective-permute-start | bytes 52232 | tf_op jit(solution)/shard_map/ppermute | solution.py:24
  38.9 4.1 copy-start.1
  38.9 4.8 copy-start.2
  56.3 6.1 %copy-start = (f32[4,34,32,129]{3,1,2,0:T(8,128)}, f32[4,34,32,129]{3,1,2,0:T(8,128)S(1)}, u32[]{:S(2)}) copy-start(f32[4,34,32,129]{3,1,2,0:T(8,128)S(1)} %get-tuple-element.38) | copy-start | bytes 6736900
  104.1 1.3 copy-start.3
  105.5 5.9 %collective-permute-start.4 = (f32[2,1,32,128]{3,1,2,0:T(1,128)S(1)}, f32[2,1,32,128]{3,1,2,0:T(1,128)S(1)}, u32[]{:S(2)}, u32[]{:S(2)}) collective-permute-start(f32[2,1,32,128]{3,1,2,0:T(1,128)S(1)} %get-tuple-element.69), channel_id=1, source_target_pairs={{0,8},{8,16},{16,24},{24,32},{32,40},{40,48},{48,56},{56,64},{64,7... | collective-permute-start | bytes 98312 | tf_op jit(solution)/shard_map/ppermute | solution.py:22
  107.3 4.4 collective-permute-start.5
  112.8 6.4 %collective-permute-start.6 = (f32[2,34,32,1]{1,2,3,0:T(8,128)S(1)}, f32[2,34,32,1]{1,2,3,0:T(8,128)S(1)}, u32[]{:S(2)}, u32[]{:S(2)}) collective-permute-start(f32[2,34,32,1]{1,2,3,0:T(8,128)S(1)} %copy.55), channel_id=1, source_target_pairs={{0,1},{1,2},{2,3},{3,4},{4,5},{5,6},{6,7},{7,0},{8,9},{9,10},{10,1... | collective-permute-start | bytes 26120 | tf_op jit(solution)/shard_map/ppermute | solution.py:22
  190.4 21.9 %all-to-all-start.1 = ((f32[2,1024,1,128]{3,2,0,1:T(1,128)}), f32[2,1024,1,128]{3,2,0,1:T(1,128)S(1)}, u32[]{:S(2)}, u32[]{:S(2)}) async-start(f32[2,1024,1,128]{3,2,0,1:T(1,128)} %copy.58), calls=%async_computation.1 | async-start | bytes 2097152 | tf_op jit(solution)/shard_map/all_to_all | solution.py:166
  353.5 6.9 %copy-start.16 = (s32[32]{0:T(128)S(1)}, s32[32]{0:T(128)}, u32[]{:S(2)}) copy-start(s32[32]{0:T(128)} %param.13) | copy-start | bytes 388
  353.5 6.9 %copy-start.15 = (s32[32]{0:T(128)S(1)}, s32[32]{0:T(128)}, u32[]{:S(2)}) copy-start(s32[32]{0:T(128)} %param.12) | copy-start | bytes 388
  354.6 30.3 %copy-start.4 = (f32[4,32,32,128]{3,1,2,0:T(8,128)S(1)}, f32[4,32,32,128]{3,1,2,0:T(8,128)}, u32[]{:S(2)}) copy-start(f32[4,32,32,128]{3,1,2,0:T(8,128)} %copy-done.3) | copy-start | bytes 6291460
  354.6 22.5 %all-to-all-start.3 = ((f32[1,1024,1,128]{3,0,2,1:T(1,128)}), f32[1,1024,1,128]{3,0,2,1:T(1,128)S(1)}, u32[]{:S(2)}, u32[]{:S(2)}) async-start(f32[1,1024,1,128]{3,0,2,1:T(1,128)} %copy.62), calls=%async_computation.3 | async-start | bytes 1048576 | tf_op jit(solution)/shard_map/all_to_all | solution.py:179
  377.1 4.3 collective-permute-start.7
  379.0 2.5 collective-permute-start.8
  381.9 2.6 collective-permute-start.9
  386.7 25.5 %all-to-all-start.4 = ((f32[1,32,32,128]{3,1,0,2:T(8,128)}), f32[1,32,32,128]{3,1,0,2:T(8,128)S(1)}, u32[]{:S(2)}, u32[]{:S(2)}) async-start(f32[1,32,32,128]{3,1,0,2:T(8,128)} %get-tuple-element.39), calls=%async_computation.4 | async-start | bytes 1048576 | tf_op jit(solution)/shard_map/all_to_all | solution.py:161
  445.7 6.6 %copy-start.13 = (f32[32,1,128]{2,1,0:T(1,128)S(1)}, f32[32,1,128]{2,1,0:T(1,128)}, u32[]{:S(2)}) copy-start(f32[32,1,128]{2,1,0:T(1,128)} %param.11) | copy-start | bytes 49156
  445.7 6.6 %copy-start.6 = (f32[32,256,128]{1,2,0:T(8,128)S(1)}, f32[32,256,128]{1,2,0:T(8,128)}, u32[]{:S(2)}) copy-start(f32[32,256,128]{1,2,0:T(8,128)} %copy.66) | copy-start | bytes 12582916
  452.3 5.0 copy-start.14
  457.3 55.9 %copy-start.8 = (f32[1,32,32,128]{3,1,2,0:T(8,128)S(1)}, f32[1,32,32,128]{3,1,2,0:T(8,128)}, u32[]{:S(2)}) copy-start(f32[1,32,32,128]{3,1,2,0:T(8,128)} %get-tuple-element.29) | copy-start | bytes 1572868
  457.3 55.9 %copy-start.9 = (f32[1,32,32,128]{3,1,2,0:T(8,128)S(1)}, f32[1,32,32,128]{3,1,2,0:T(8,128)}, u32[]{:S(2)}) copy-start(f32[1,32,32,128]{3,1,2,0:T(8,128)} %get-tuple-element.30) | copy-start | bytes 1572868
  457.3 55.9 %copy-start.10 = (f32[1,32,32,128]{3,1,2,0:T(8,128)S(1)}, f32[1,32,32,128]{3,1,2,0:T(8,128)}, u32[]{:S(2)}) copy-start(f32[1,32,32,128]{3,1,2,0:T(8,128)} %get-tuple-element.40) | copy-start | bytes 1572868
  508.1 22.2 %all-to-all-start.5 = ((f32[1,1024,1,128]{3,2,0,1:T(1,128)}), f32[1,1024,1,128]{3,2,0,1:T(1,128)S(1)}, u32[]{:S(2)}, u32[]{:S(2)}) async-start(f32[1,1024,1,128]{3,2,0,1:T(1,128)} %bitcast.44), calls=%async_computation.5 | async-start | bytes 1048576 | tf_op jit(solution)/shard_map/all_to_all | solution.py:180
  513.4 2.1 copy-start.7
where the time goes:
time: 542 us; the launch traced here: 532 us
  matrix products  171 us (32%)
  local copies, waits for them, and re-layouts  103 us (19%)
  other arithmetic  92.4 us (17%)
  waiting for transfers between devices  73.5 us (14%)
  blocking collectives  47.4 us (9%)
  starting transfers between devices  42.8 us (8%)
    dot_general x8, matrix products, transform_axis(): jnp.einsum(einsum_forms[which_axis], table, spectrum, precision=lax.Preci...  159 us
    scatter-add x1, other arithmetic, render(): gradient = jnp.zeros((grid_x, pixels), jnp.float32).at[cell_index.reshape...  45.1 us
    gather x2, local copies, waits for them, and re-layouts, render(): samples = jnp.take(flat_density, cell_index, axis=0)  33.5 us
    add x1, other arithmetic, shards(): summed = summed + weight_x[slot_x] * weight_y[slot_y] * z_summed  30.8 us
    all_to_all x1, blocking collectives, shards(): lax.all_to_all(divergence[None], 'sim', split_axis=2, concat_axis=1, tile...  28.4 us
    slice x3, local copies, waits for them, and re-layouts, shards(): z_summed = z_summed + weight_z[slot_z] * jnp.roll(shifted, -shift_z, axis=2)  21.1 us
    all_to_all x1, blocking collectives, shards(): lax.all_to_all(spectrum, 'pen', split_axis=3, concat_axis=1, tiled=True)  19 us
    all_to_all x1, waiting for transfers between devices, shards(): lax.all_to_all(spectrum, 'pen', split_axis=1, concat_axis=3, tiled=True)  16.9 us
  transfers between devices with their start and end apart: 14, of which 9 were waited for; matrix products, arithmetic and copies ran while one was open for 6% of the time, Pallas kernels for 0%

commit v1 on v0

v1 whole, which is shorter than its diff:
```python
import functools

import jax
import jax.numpy as jnp
import numpy as np
from jax import lax
from jax.experimental import pallas as pl
from jax.experimental.pallas import tpu as pltpu
from jax.sharding import PartitionSpec as P

STEPS = 256
ABSORB = 2.0 / STEPS
LANES = 128
SEGMENTS = 8
MSG = 144
f32 = jnp.float32
bf16 = jnp.bfloat16


def hartley_pieces(length):
    index = np.arange(length)
    angles = (np.outer(index, index) % length) * (2.0 * np.pi / length)
    table = (np.cos(angles) + np.sin(angles)) / np.sqrt(length)
    pieces = []
    for _ in range(3):
        piece = table.astype(jnp.bfloat16)
        pieces.append(piece)
        table = table - piece.astype(np.float64)
    return np.stack(pieces)


def line_tables(length_y, length_x, local_x, layers):
    eig = 4.0 * np.sin(np.pi * np.arange(length_y) / length_y) ** 2
    half = eig / 2.0
    root = 1.0 / (1.0 + half + np.sqrt(half * (half + 2.0)))
    gap = 1.0 / root - root
    gap[0] = 1.0
    forward = -1.0 / gap
    backward = -1.0 / gap
    forward[0] = 1.0
    backward[0] = 0.0
    block = root**local_x
    closing = 1.0 - root**length_x
    closing[0] = 1.0
    closing = 1.0 / closing
    closing[0] = 0.0
    rows = np.stack([root, 1.0 / root, forward, backward, block, closing])
    rows = rows.reshape(6, length_y // LANES, 1, LANES)
    return np.repeat(rows, layers, axis=2).reshape(6, -1, LANES).astype(np.float32)


def split_two(values):
    high = values.astype(bf16)
    low = (values - high.astype(f32)).astype(bf16)
    return high, low


def split_three(values):
    high = values.astype(bf16)
    rest = values - high.astype(f32)
    mid = rest.astype(bf16)
    low = (rest - mid.astype(f32)).astype(bf16)
    return high, mid, low


def iota(shape, dim):
    return lax.broadcasted_iota(jnp.int32, shape, dim)


def matmul(a, b):
    return jnp.dot(a, b, preferred_element_type=f32)


def step_kernel(
    sizes,
    dens, vel, code, frac, targ, vstart, vsign, tables_hbm, lines,
    o_dens, o_vel, o_img, o_grad,
    ext, pack, xlo, xhi, pin, dens_k, ax_k, ay_k,
    rays, d_send, d_in, x_pieces, q_tab, spec, spec_end,
    c_send, c_in, c_out, c_ret, p_spec, y_pieces, o_send, o_in,
    prefix, w_light, v_light, gathered, rhs, sums, g_send, g_in,
    halo_s, halo_r, dens_s, dens_r, d_s, d_r, c_s, c_r, b_s, b_r, o_s, o_r, g_s, g_r, tab_sem,
):
    S, N, LX, K, VIEWS = sizes
    KP = K // N
    NX, NY = S * LX, N * LANES
    ROWS = KP * LX
    SEG = NX // SEGMENTS
    me = lax.axis_index("sim")
    pe = lax.axis_index("pen")

    def simp(off):
        return lax.rem(me + off + S, S)

    def penp(off):
        return lax.rem(pe + off + N, N)

    table_copies = [pltpu.make_async_copy(tables_hbm.at[t], q_tab.at[t], tab_sem.at[t]) for t in range(3)]
    for copy in table_copies:
        copy.start()

    barrier = pltpu.get_barrier_semaphore()

    def greet_sim(off, _):
        pl.semaphore_signal(barrier, inc=1, device_id={"sim": simp(off), "pen": pe}, device_id_type=pl.DeviceIdType.MESH)
        return 0

    def greet_pen(off, _):
        pl.semaphore_signal(barrier, inc=1, device_id={"sim": me, "pen": penp(off)}, device_id_type=pl.DeviceIdType.MESH)
        return 0

    lax.fori_loop(1, S, greet_sim, 0)
    lax.fori_loop(1, N, greet_pen, 0)
    corners = ((-1, -1), (-1, 1), (1, -1), (1, 1))
    for dx, dy in corners:
        pl.semaphore_signal(barrier, inc=1, device_id={"sim": simp(dx), "pen": penp(dy)}, device_id_type=pl.DeviceIdType.MESH)

    lane = iota((K, LANES), 1)

    def source(field, x):
        return dens[x] if field == 0 else vel[field - 1, x]

    def pack_body(x, carry):
        first, last = carry
        for field in range(4):
            cells = source(field, x)
            spot = field * LX + x
            here = lane == spot
            first = jnp.where(here, pltpu.roll(cells, spot, 1), first)
            last = jnp.where(here, pltpu.roll(cells, lax.rem(spot + 1, LANES), 1), last)
        return first, last

    nothing = jnp.zeros((K, LANES), f32)
    first, last = lax.fori_loop(0, LX, pack_body, (nothing, nothing))
    pack[0] = first
    pack[1] = last
    for field in range(4):
        pack[2 + field] = source(field, 0)
        pack[6 + field] = source(field, LX - 1)

    pl.semaphore_wait(barrier, (S - 1) + (N - 1) + 4)

    def remote(src, dst, s_sem, r_sem, sim, pen):
        return pltpu.make_async_remote_copy(
            src_ref=src, dst_ref=dst, send_sem=s_sem, recv_sem=r_sem,
            device_id={"sim": sim, "pen": pen}, device_id_type=pl.DeviceIdType.MESH,
        )

    halo = [
        remote(pack.at[pl.ds(6, 4)], xlo, halo_s.at[0], halo_r.at[0], simp(1), pe),
        remote(pack.at[pl.ds(2, 4)], xhi, halo_s.at[1], halo_r.at[1], simp(-1), pe),
    ]
    for side in range(2):
        for dx in (-1, 0, 1):
            slot = side * 3 + 1 + dx
            halo.append(
                remote(
                    pack.at[1 - side], pin.at[slot], halo_s.at[2 + slot], halo_r.at[2 + slot],
                    simp(-dx), penp(1 if side == 0 else -1),
                )
            )
    for copy in halo:
        copy.start()

    def spread_body(x, _):
        for field in range(4):
            cells = source(field, x)
            ext[0, field, x + 1] = pltpu.roll(cells, 1, 1)
            ext[1, field, x + 1] = cells
            ext[2, field, x + 1] = pltpu.roll(cells, LANES - 1, 1)
        return 0

    lax.fori_loop(0, LX, spread_body, 0)
    for copy in halo:
        copy.wait()

    is_first = lane == 0
    is_last = lane == LANES - 1

    def fix_body(x, _):
        for field in range(4):
            spot = field * LX + x
            left = pltpu.roll(pin[1], LANES - spot, 1)
            right = pltpu.roll(pin[4], LANES - 1 - spot, 1)
            ext[0, field, x + 1] = jnp.where(is_first, left, ext[0, field, x + 1])
            ext[2, field, x + 1] = jnp.where(is_last, right, ext[2, field, x + 1])
        return 0

    lax.fori_loop(0, LX, fix_body, 0)
    for row, rows, slot, at in ((0, xlo, 0, LX - 1), (LX + 1, xhi, 2, 0)):
        for field in range(4):
            spot = field * LX + at
            cells = rows[field]
            left = pltpu.roll(pin[slot], (LANES - spot) % LANES, 1)
            right = pltpu.roll(pin[3 + slot], LANES - 1 - spot, 1)
            ext[0, field, row] = jnp.where(is_first, left, pltpu.roll(cells, 1, 1))
            ext[1, field, row] = cells
            ext[2, field, row] = jnp.where(is_last, right, pltpu.roll(cells, LANES - 1, 1))

    def weights(bit, fraction):
        rest = 1.0 - fraction
        on = bit == 1
        return (jnp.where(on, rest, 0.0), jnp.where(on, fraction, rest), jnp.where(on, 0.0, fraction))

    def advect_body(x, _):
        codes = code[x]
        wx = weights(codes & 1, frac[0, x])
        wz = weights((codes >> 1) & 1, frac[1, x])
        wy = weights((codes >> 2) & 1, frac[2, x])
        totals = [None] * 4
        for slot, shift in ((1, 0), (0, -1), (2, 1)):
            if shift == 0:
                rx, ry = wx, wy
            else:
                amount = shift % K
                rx = [pltpu.roll(w, amount, 0) for w in wx]
                ry = [pltpu.roll(w, amount, 0) for w in wy]
            for field in range(4):
                term = None
                for sy in range(3):
                    part = (
                        rx[0] * ext[sy, field, x]
                        + rx[1] * ext[sy, field, x + 1]
                        + rx[2] * ext[sy, field, x + 2]
                    )
                    term = ry[sy] * part if term is None else term + ry[sy] * part
                if shift != 0:
                    term = pltpu.roll(term, (-shift) % K, 0)
                term = wz[slot] * term
                totals[field] = term if totals[field] is None else totals[field] + term
        o_dens[pl.ds(pl.multiple_of(x * K, 8), K), :] = totals[0]
        o_vel[pl.ds(pl.multiple_of(LX * K + x * K, 8), K), :] = totals[2]
        dens_k[pl.ds(x, K, stride=LX), :] = totals[0]
        ax_k[pl.ds(x, K, stride=LX), :] = totals[1]
        ay_k[pl.ds(x, K, stride=LX), :] = totals[3]
        return 0

    lax.fori_loop(0, LX, advect_body, 0)

    def sim_exchange(src, src_rows, dst, s_sem, r_sem):
        def descriptor(peer, start_at):
            a = src.at[pl.ds(pl.multiple_of(peer * src_rows, 8), src_rows)]
            b = dst.at[pl.ds(pl.multiple_of(start_at * src_rows, 8), src_rows)]
            return remote(a, b, s_sem.at[peer], r_sem.at[start_at], peer, pe)

        def start():
            def body(off, _):
                descriptor(simp(off), me).start()
                return 0

            lax.fori_loop(1, S, body, 0)

        def wait_recv():
            def body(off, _):
                peer = simp(off)
                descriptor(peer, peer).wait_recv()
                return 0

            lax.fori_loop(1, S, body, 0)

        def wait_send():
            def body(off, _):
                descriptor(simp(off), me).wait_send()
                return 0

            lax.fori_loop(1, S, body, 0)

        return start, wait_recv, wait_send

    def pen_exchange(src, dst, s_sem, r_sem):
        def descriptor(peer, start_at):
            return remote(src.at[peer], dst.at[start_at], s_sem.at[peer], r_sem.at[start_at], me, peer)

        def loop(method, swap):
            def body(off, _):
                peer = penp(off)
                getattr(descriptor(peer, peer if swap else pe), method)()
                return 0

            lax.fori_loop(1, N, body, 0)

        return (lambda: loop("start", False)), (lambda: loop("wait_recv", True)), (lambda: loop("wait_send", False))

    dens_x = sim_exchange(dens_k, LX, rays, dens_s, dens_r)
    dens_x[0]()
    mine = pl.ds(pl.multiple_of(me * LX, 8), LX)
    rays[mine, :] = dens_k[mine, :]

    sub_x = iota((LX, LANES), 0)
    lane_x = iota((LX, LANES), 1)

    def div_body(part, _):
        base = part * ROWS
        ends = []
        for layer in range(KP):
            at = pl.ds(pl.multiple_of(base + layer * LX, 8), LX)
            ax = ax_k[at, :]
            ay = ay_k[at, :]
            before_x = jnp.where(sub_x == 0, 0.0, pltpu.roll(ax, 1, 0))
            before_y = jnp.where(lane_x == 0, 0.0, pltpu.roll(ay, 1, 1))
            d_send[part, layer * LX : (layer + 1) * LX, :] = (ax - before_x) + (ay - before_y)
            ends.append(-ax[LX - 1 : LX, :])
        d_send[part, ROWS : ROWS + 8, :] = jnp.concatenate(ends + [jnp.zeros((8 - KP, LANES), f32)], axis=0)
        turned = jnp.transpose(ay_k[pl.ds(pl.multiple_of(base, 8), ROWS), :])
        d_send[part, ROWS + 8 : ROWS + 16, :] = jnp.broadcast_to(turned[LANES - 1 : LANES, :], (8, ROWS))
        return 0

    lax.fori_loop(0, N, div_body, 0)
    d_x = pen_exchange(d_send, d_in, d_s, d_r)
    d_x[0]()
    d_in[pe] = d_send[pe]
    for copy in table_copies:
        copy.wait()
    d_x[1]()

    lane_r = iota((ROWS, LANES), 1)
    for part in range(N):
        cells = d_in[part, 0:ROWS, :]
        row = d_in[(part - 1) % N, ROWS + 8 : ROWS + 9, :]
        column = jnp.transpose(jnp.broadcast_to(row, (LANES, ROWS)))
        cells = cells - jnp.where(lane_r == 0, column, 0.0)
        at = slice(part * LANES, (part + 1) * LANES)
        high, low = split_two(cells)
        x_pieces[0, 0:ROWS, at] = high
        x_pieces[1, 0:ROWS, at] = low
        high, low = split_two(d_in[part, ROWS:MSG, :])
        x_pieces[0, ROWS:MSG, at] = high
        x_pieces[1, ROWS:MSG, at] = low

    wide = 2 * LANES

    def forward_body(n, _):
        at = pl.ds(pl.multiple_of(n * wide, wide), wide)
        q0, q1 = q_tab[0, :, at], q_tab[1, :, at]
        result = matmul(x_pieces[0], q0) + (matmul(x_pieces[0], q1) + matmul(x_pieces[1], q0))
        for half in range(2):
            columns = result[:, half * LANES : (half + 1) * LANES]
            spec[pl.ds(pl.multiple_of((2 * n + half) * ROWS, 8), ROWS), :] = columns[0:ROWS]
            spec_end[2 * n + half] = columns[ROWS : ROWS + 8]
        return 0

    lax.fori_loop(0, NY // wide, forward_body, 0)

    LINES = N * KP
    root = lines[0]
    root_inv = lines[1]
    beyond = jnp.concatenate([spec_end[part, 0:KP, :] for part in range(N)], axis=0)
    flat = jnp.zeros((LINES, LANES), f32)

    def at_x(x):
        return pl.ds(x, LINES, stride=LX)

    def ends_body(i, carry):
        fwd, bwd, acc = carry
        fwd = spec[at_x(i), :] + root * fwd
        acc = acc + fwd
        bwd = root * (spec[at_x(LX - 1 - i), :] + bwd)
        return fwd, bwd, acc

    fwd, bwd, acc = lax.fori_loop(0, LX, ends_body, (flat, root * beyond, flat), unroll=2)
    fwd = fwd + root_inv * beyond

    def carry_row(row):
        return pl.ds(row, LINES, stride=8)

    c_send[carry_row(0), :] = fwd
    c_send[carry_row(1), :] = bwd
    c_send[carry_row(2), :] = acc
    for row in range(3, 8):
        c_send[carry_row(row), :] = flat
    c_x = sim_exchange(c_send, 8, c_in, c_s, c_r)
    c_x[0]()
    my_carry = pl.ds(pl.multiple_of(me * 8, 8), 8)
    c_in[my_carry, :] = c_send[my_carry, :]

    dens_x[1]()

    def strided(x):
        return pl.ds(x, SEGMENTS, stride=SEG)

    def chain(x):
        return pl.ds(pl.multiple_of(x * SEGMENTS, SEGMENTS), SEGMENTS)

    seg0 = jnp.zeros((SEGMENTS, LANES), f32)

    def scan_body(i, carry):
        depth, down, up = carry
        back = SEG - 1 - i
        glow = ABSORB * rays[strided(i), :]
        prefix[chain(i), :] = depth
        depth = depth + glow
        down = glow + jnp.exp(-glow) * down
        v_light[chain(i), :] = down
        glow_b = ABSORB * rays[strided(back), :]
        up = glow_b + jnp.exp(-glow_b) * up
        w_light[chain(back), :] = up
        return depth, down, up

    seg_depth, seg_down, seg_up = lax.fori_loop(0, SEG, scan_body, (seg0, seg0, seg0), unroll=4)
    seg_pass = jnp.exp(-seg_depth)
    one = jnp.zeros((1, LANES), f32)
    total_depth, run_down, run_up = one, one, one
    starts = []
    for g in range(SEGMENTS):
        starts.append(total_depth)
        total_depth = total_depth + seg_depth[g : g + 1, :]
        run_down = seg_down[g : g + 1, :] + seg_pass[g : g + 1, :] * run_down
        h = SEGMENTS - 1 - g
        run_up = seg_up[h : h + 1, :] + seg_pass[h : h + 1, :] * run_up
    total_pass = jnp.exp(-total_depth)
    closing = 1.0 / (1.0 - total_pass)
    run_down = run_down * closing
    run_up = run_up * closing
    downs, ups = [], []
    for g in range(SEGMENTS):
        downs.append(run_down)
        run_down = seg_down[g : g + 1, :] + seg_pass[g : g + 1, :] * run_down
        h = SEGMENTS - 1 - g
        ups.append(run_up)
        run_up = seg_up[h : h + 1, :] + seg_pass[h : h + 1, :] * run_up
    start_depth = jnp.concatenate(starts, axis=0)
    down_in = jnp.concatenate(downs, axis=0)
    up_in = jnp.concatenate(ups[::-1], axis=0)

    def finish_body(i, _):
        glow = ABSORB * rays[strided(i), :]
        depth = prefix[chain(i), :]
        v_light[chain(i), :] = v_light[chain(i), :] + jnp.exp(-(depth + glow)) * down_in
        w_light[chain(i), :] = w_light[chain(i), :] + jnp.exp(depth - seg_depth) * up_in
        prefix[chain(i), :] = depth + start_depth
        return 0

    lax.fori_loop(0, SEG, finish_body, 0, unroll=4)

    c_x[1]()
    block = lines[4, pl.ds(me, 1), :]
    close = lines[5, pl.ds(me, 1), :]
    lone = jnp.logical_and(iota((1, LANES), 1) == 0, me < KP)

    def carry_at(i, row):
        return pl.ds(8 * i + row, 1)

    def around_body(i, carry):
        a, b = carry
        a = c_in[carry_at(i, 0), :] + block * a
        b = c_in[carry_at(S - 1 - i, 1), :] + block * b
        return a, b

    a, b = lax.fori_loop(0, S, around_body, (one, one))

    def carry_body(i, carry):
        a, b, total = carry
        j = S - 1 - i
        c_out[carry_at(i, 0), :] = a
        c_out[carry_at(j, 1), :] = b
        total = total + (c_in[carry_at(i, 2), :] + LX * a)
        return c_in[carry_at(i, 0), :] + block * a, c_in[carry_at(j, 1), :] + block * b, total

    _, _, total = lax.fori_loop(0, S, carry_body, (a * close, b * close, one))
    mean = total * (1.0 / NX)

    def lone_body(i, offset):
        slope = c_out[carry_at(i, 0), :] - mean
        c_out[carry_at(i, 0), :] = jnp.where(lone, slope, c_out[carry_at(i, 0), :])
        c_out[carry_at(i, 1), :] = jnp.where(lone, offset, c_out[carry_at(i, 1), :])
        return offset + (c_in[carry_at(i, 2), :] + LX * slope)

    lax.fori_loop(0, S, lone_body, one)
    for row in range(2, 8):
        c_out[carry_row(row), :] = flat
    b_x = sim_exchange(c_out, 8, c_ret, b_s, b_r)
    b_x[0]()
    c_ret[my_carry, :] = c_out[my_carry, :]

    sub_v = iota((VIEWS, LANES), 0)
    lane_m = iota((1, 6 * VIEWS), 1)
    view_m = lax.rem(lane_m, VIEWS)

    def where_is(x):
        return lax.rem(x, SEG) * SEGMENTS + lax.div(x, SEG)

    def view_body(v, carry):
        ups_v, start_m, up_m = carry
        x0 = vstart[v]
        up = vsign[v] == 1
        far = jnp.where(up, x0 + STEPS, x0 - STEPS)
        wraps = jnp.logical_or(far >= NX, far < 0)
        xe = jnp.where(far >= NX, far - NX, jnp.where(far < 0, far + NX, far))
        out = []
        for x in (x0, xe):
            at = pl.ds(where_is(x), 1)
            depth = prefix[at, :]
            depth = jnp.where(up, depth, -(depth + ABSORB * rays[pl.ds(x, 1), :]))
            out.append((depth, jnp.where(up, w_light[at, :], v_light[at, :])))
        gathered[0, pl.ds(v, 1), :] = out[0][0]
        gathered[1, pl.ds(v, 1), :] = out[0][1]
        gathered[2, pl.ds(v, 1), :] = out[1][0] + jnp.where(wraps, total_depth, 0.0)
        gathered[3, pl.ds(v, 1), :] = out[1][1]
        flag = vsign[v]
        return (
            jnp.where(sub_v == v, flag, ups_v),
            jnp.where(view_m == v, x0, start_m),
            jnp.where(view_m == v, flag, up_m),
        )

    none_m = jnp.zeros((1, 6 * VIEWS), jnp.int32)
    ups_v, start_m, up_m = lax.fori_loop(0, VIEWS, view_body, (jnp.zeros((VIEWS, LANES), jnp.int32), none_m, none_m))
    entry, light0, leave, light1 = gathered[0], gathered[1], gathered[2], gathered[3]
    seen_through = jnp.exp(entry - leave) * light1
    picture = light0 - seen_through
    o_img[:, 0, :] = picture
    pull = (STEPS * ABSORB) * (picture - targ[:, 0, :])
    coef = pull * jnp.exp(entry)
    alpha = jnp.where(ups_v == 1, coef, 0.0)
    gamma = jnp.where(ups_v == 1, 0.0, coef)
    beta = pull * seen_through
    for slot, value in enumerate((alpha, gamma, beta)):
        wrapped = beta if slot == 2 else value * total_pass
        both = jnp.concatenate([value, wrapped], axis=0)
        for t, piece in enumerate(split_three(both)):
            rhs[t * 2 * VIEWS : (t + 1) * 2 * VIEWS, slot * LANES : (slot + 1) * LANES] = piece

    kind = lax.rem(lax.div(lane_m, VIEWS), 2) == 1
    tile = 256

    def window_body(n, _):
        row = n * tile + iota((tile, 6 * VIEWS), 0)
        x = lax.rem(row, SEGMENTS) * SEG + lax.div(row, SEGMENTS)
        delta = jnp.where(up_m == 1, x - start_m, start_m - x)
        back = delta < 0
        inside = jnp.where(back, delta + NX, delta) < STEPS
        chosen = jnp.logical_and(inside, jnp.logical_xor(back, jnp.logical_not(kind)))
        mask = jnp.where(chosen, 1.0, 0.0).astype(bf16)
        sums[pl.ds(pl.multiple_of(n * tile, tile), tile), :] = matmul(mask, rhs[...])
        return 0

    lax.fori_loop(0, NX // tile, window_body, 0)

    def grad_body(i, _):
        glow = ABSORB * rays[strided(i), :]
        depth = prefix[chain(i), :]
        terms = sums[chain(i), :]
        g_send[strided(i), :] = (
            jnp.exp(-depth) * (1.0 - w_light[chain(i), :] + glow) * terms[:, 0:LANES]
            + jnp.exp(depth + glow) * (1.0 - v_light[chain(i), :] + glow) * terms[:, LANES : 2 * LANES]
            + terms[:, 2 * LANES : 3 * LANES]
        )
        return 0

    lax.fori_loop(0, SEG, grad_body, 0, unroll=4)
    g_x = sim_exchange(g_send, LX, g_in, g_s, g_r)
    g_x[0]()
    g_in[mine, :] = g_send[mine, :]

    b_x[1]()
    factor_f = lines[2]
    factor_b = lines[3]
    alone = jnp.logical_and(iota((LINES, LANES), 1) == 0, iota((LINES, LANES), 0) < KP)
    first_f = c_ret[carry_row(0), :]
    tail = c_ret[carry_row(1), :]
    back_in = tail + root * beyond

    def back_body(i, bwd):
        x = LX - 1 - i
        p_spec[at_x(x), :] = factor_b * bwd
        return root * (spec[at_x(x), :] + bwd)

    lax.fori_loop(0, LX, back_body, back_in, unroll=2)

    def front_body(x, carry):
        fwd, height = carry
        fwd = spec[at_x(x), :] + root * fwd
        p_spec[at_x(x), :] = p_spec[at_x(x), :] + factor_f * jnp.where(alone, height, fwd)
        return fwd, height + fwd

    fwd, height = lax.fori_loop(0, LX, front_body, (first_f, tail), unroll=2)
    after = factor_f * jnp.where(alone, height, root * fwd) + factor_b * (root_inv * back_in)
    for part in range(N):
        at = slice(part * LANES, (part + 1) * LANES)
        for t, piece in enumerate(split_three(p_spec[part * ROWS : (part + 1) * ROWS, :])):
            y_pieces[t, 0:ROWS, at] = piece
        end = jnp.concatenate([after[part * KP : (part + 1) * KP], jnp.zeros((MSG - ROWS - KP, LANES), f32)], axis=0)
        for t, piece in enumerate(split_three(end)):
            y_pieces[t, ROWS:MSG, at] = piece

    def inverse_body(n, _):
        at = pl.ds(pl.multiple_of(n * wide, wide), wide)
        q0, q1, q2 = q_tab[0, :, at], q_tab[1, :, at], q_tab[2, :, at]
        y0, y1, y2 = y_pieces[0], y_pieces[1], y_pieces[2]
        small = matmul(y1, q1) + matmul(y0, q2) + matmul(y2, q0)
        result = matmul(y0, q0) + (matmul(y1, q0) + matmul(y0, q1) + small)
        o_send[2 * n, :, :] = result[:, 0:LANES]
        o_send[2 * n + 1, :, :] = result[:, LANES:wide]
        return 0

    lax.fori_loop(0, NY // wide, inverse_body, 0)
    for part in range(N):
        turned = jnp.transpose(o_send[(part + 1) % N, 0:ROWS, :])
        o_send[part, ROWS + 8 : ROWS + 16, :] = jnp.broadcast_to(turned[0:1, :], (8, ROWS))
    o_x = pen_exchange(o_send, o_in, o_s, o_r)
    o_x[0]()
    o_in[pe] = o_send[pe]
    o_x[1]()

    def velocity_body(part, _):
        column = jnp.transpose(jnp.broadcast_to(o_in[part, ROWS + 8 : ROWS + 9, :], (LANES, ROWS)))
        for layer in range(KP):
            k = part * KP + layer
            at = pl.ds(pl.multiple_of(k * LX, 8), LX)
            here = o_in[part, layer * LX : (layer + 1) * LX, :]
            above = o_in[part, ROWS + layer : ROWS + layer + 1, :]
            next_x = jnp.where(sub_x == LX - 1, above, pltpu.roll(here, LX - 1, 0))
            next_y = jnp.where(
                lane_x == LANES - 1, column[layer * LX : (layer + 1) * LX, :], pltpu.roll(here, LANES - 1, 1)
            )
            o_vel[pl.ds(k, LX, stride=K), :] = ax_k[at, :] - (next_x - here)
            o_vel[pl.ds(2 * LX * K + k, LX, stride=K), :] = ay_k[at, :] - (next_y - here)
        return 0

    lax.fori_loop(0, N, velocity_body, 0)

    g_x[1]()

    def back_home(k, _):
        o_grad[pl.ds(k, LX, stride=K), :] = g_in[pl.ds(pl.multiple_of(k * LX, 8), LX), :]
        return 0

    lax.fori_loop(0, K, back_home, 0)
    for copy_sends in (dens_x[2], d_x[2], c_x[2], b_x[2], g_x[2], o_x[2]):
        copy_sends()


def solution(mesh):
    S, N = mesh.shape["sim"], mesh.shape["pen"]

    def shards(density, velocity, stencil_code, fractions, targets, view_start, view_sign):
        LX, K, LY = density.shape
        VIEWS = targets.shape[0]
        NX, NY = LX * S, LY * N
        tables = jnp.asarray(hartley_pieces(NY))
        lines = jnp.asarray(line_tables(NY, NX, LX, K // N))
        vmem = pl.BlockSpec(memory_space=pltpu.VMEM)
        smem = pl.BlockSpec(memory_space=pltpu.SMEM)
        dma = pltpu.SemaphoreType.DMA
        scratch = [
            pltpu.VMEM((3, 4, LX + 2, K, LY), f32),
            pltpu.VMEM((10, K, LY), f32),
            pltpu.VMEM((4, K, LY), f32),
            pltpu.VMEM((4, K, LY), f32),
            pltpu.VMEM((6, K, LY), f32),
            pltpu.VMEM((K * LX, LY), f32),
            pltpu.VMEM((K * LX, LY), f32),
            pltpu.VMEM((K * LX, LY), f32),
            pltpu.VMEM((NX, LY), f32),
            pltpu.VMEM((N, MSG, LY), f32),
            pltpu.VMEM((N, MSG, LY), f32),
            pltpu.VMEM((2, MSG, NY), bf16),
            pltpu.VMEM((3, NY, NY), bf16),
            pltpu.VMEM((N * 128, LANES), f32),
            pltpu.VMEM((N, 8, LANES), f32),
            pltpu.VMEM((S * 8, LANES), f32),
            pltpu.VMEM((S * 8, LANES), f32),
            pltpu.VMEM((S * 8, LANES), f32),
            pltpu.VMEM((S * 8, LANES), f32),
            pltpu.VMEM((N * 128, LANES), f32),
            pltpu.VMEM((3, MSG, NY), bf16),
            pltpu.VMEM((N, MSG, LY), f32),
            pltpu.VMEM((N, MSG, LY), f32),
            pltpu.VMEM((NX, LY), f32),
            pltpu.VMEM((NX, LY), f32),
            pltpu.VMEM((NX, LY), f32),
            pltpu.VMEM((4, VIEWS, LY), f32),
            pltpu.VMEM((6 * VIEWS, 3 * LY), bf16),
            pltpu.VMEM((NX, 3 * LY), f32),
            pltpu.VMEM((NX, LY), f32),
            pltpu.VMEM((K * LX, LY), f32),
            dma((8,)), dma((8,)),
            dma((S,)), dma((S,)),
            dma((N,)), dma((N,)),
            dma((S,)), dma((S,)),
            dma((S,)), dma((S,)),
            dma((N,)), dma((N,)),
            dma((S,)), dma((S,)),
            dma((3,)),
        ]
        density_new, velocity_new, images, gradient = pl.pallas_call(
            functools.partial(step_kernel, (S, N, LX, K, VIEWS)),
            out_shape=(
                jax.ShapeDtypeStruct((LX * K, LY), f32),
                jax.ShapeDtypeStruct((3 * LX * K, LY), f32),
                jax.ShapeDtypeStruct(targets.shape, f32),
                jax.ShapeDtypeStruct((LX * K, LY), f32),
            ),
            in_specs=[vmem, vmem, vmem, vmem, vmem, smem, smem, pl.BlockSpec(memory_space=pl.ANY), vmem],
            out_specs=(vmem, vmem, vmem, vmem),
            scratch_shapes=scratch,
            compiler_params=pltpu.CompilerParams(
                collective_id=0, has_side_effects=True, vmem_limit_bytes=60 * 1024 * 1024
            ),
        )(density, velocity, stencil_code, fractions, targets, view_start, view_sign, tables, lines)
        return (
            density_new.reshape(LX, K, LY),
            velocity_new.reshape(3, LX, K, LY),
            images,
            gradient.reshape(LX, K, LY),
        )

    return jax.shard_map(
        shards,
        mesh=mesh,
        in_specs=(
            P("sim", None, "pen"),
            P(None, "sim", None, "pen"),
            P("sim", None, "pen"),
            P(None, "sim", None, "pen"),
            P(None, "sim", "pen"),
            P(),
            P(),
        ),
        out_specs=(
            P("sim", None, "pen"),
            P(None, "sim", None, "pen"),
            P(None, "sim", "pen"),
            P("sim", None, "pen"),
        ),
        check_vma=False,
    )
```

time: 542 us -> 91.1 us (0.17); the launches traced: 532 us -> 91 us
  matrix products: 171 us -> 0 us
  local copies, waits for them, and re-layouts: 103 us -> 6 us
  other arithmetic: 92.4 us -> 0 us
  Pallas kernels: 0 us -> 84.3 us
  waiting for transfers between devices: 73.5 us -> 0 us
  blocking collectives: 47.4 us -> 0 us
  starting transfers between devices: 42.8 us -> 0 us
    dot_general x10 -> x0, matrix products: 171 us -> none  [the longest x8 159 us: transform_axis(): jnp.einsum(einsum_forms[which_axis], table, spectrum, precision=lax.Preci...]
    pallas_call x0 -> x1, Pallas kernels: none -> 84.3 us  [shards(): pl.pallas_call(functools.partial(step_kernel, (S, N, LX, K, VIEWS)), out_...]
    all_to_all x4 -> x0, waiting for transfers between devices: 63.7 us -> none  [the longest x1 16.9 us: shards(): lax.all_to_all(spectrum, 'pen', split_axis=1, concat_axis=3, tiled=True)]
    all_to_all x2 -> x0, blocking collectives: 47.4 us -> none  [the longest x1 28.4 us: shards(): lax.all_to_all(divergence[None], 'sim', split_axis=2, concat_axis=1, tile...]
    scatter-add x1 -> x0, other arithmetic: 45.1 us -> none  [render(): gradient = jnp.zeros((grid_x, pixels), jnp.float32).at[cell_index.reshape...]
    gather x2 -> x0, local copies, waits for them, and re-layouts: 33.5 us -> none  [render(): samples = jnp.take(flat_density, cell_index, axis=0)]
    add x3 -> x0, other arithmetic: 31.2 us -> none  [the longest x1 30.8 us: shards(): summed = summed + weight_x[slot_x] * weight_y[slot_y] * z_summed]
    slice x10 -> x0, local copies, waits for them, and re-layouts: 31.2 us -> none  [the longest x3 21.1 us: shards(): z_summed = z_summed + weight_z[slot_z] * jnp.roll(shifted, -shift_z, axis=2)]
  transfers between devices with their start and end apart: 14 -> 0, of which waited for: 9 -> 0; matrix products, arithmetic and copies ran while one was open for 6% -> 0% of each run, Pallas kernels for 0% -> 0%
where the time goes in v1:
time: 91.1 us; the launch traced here: 91 us
  Pallas kernels  84.3 us (93%)
  local copies, waits for them, and re-layouts  6 us (7%)
    pallas_call x1, Pallas kernels, shards(): pl.pallas_call(functools.partial(step_kernel, (S, N, LX, K, VIEWS)), out_...  84.3 us
    unnamed x8, local copies, waits for them, and re-layouts  6 us

profile of v1, /device:TPU:1, one launch (start us, length us, event | category | flops | bytes accessed | tf_op | source)
XLA Modules:
  0.0 91.0 jit_solution(6808947373227617370)
XLA Ops:
  0.6 84.3 %shard_map.120 = (f32[1024,128]{1,0:T(8,128)}, f32[3072,128]{1,0:T(8,128)}, f32[32,1,128]{2,1,0:T(1,128)}, f32[1024,128]{1,0:T(8,128)}) custom-call(f32[32,32,128]{2,1,0:T(8,128)} %dens.1, f32[3,32,32,128]{3,2,1,0:T(8,128)} %vel.1, s32[32,32,128]{2,1,0:T(8,128)} %code.1, f32[3,32,32,128]{3,2,1,0:T(8,128)} %frac.1, f32[32,1,128]{2,1,0:T(1,128)} %targ.1, ...), custom_call_target="tpu_custom_call" | custom-call | tf_op jit(solution)/shard_map/pallas_call | solution.py:686
  85.0 1.9 %copy.17 = f32[32,32,128]{2,1,0:T(8,128)} copy(f32[32,32,128]{2,1,0:T(8,128)} %bitcast.5) | data formatting | bytes 1048576
  86.8 0.0 copy-start.1
  86.8 0.0 copy-start
  86.8 2.7 %copy.18 = f32[3,32,32,128]{3,2,1,0:T(8,128)} copy(f32[3,32,32,128]{3,2,1,0:T(8,128)} %bitcast.3) | data formatting | bytes 3145728
  89.6 0.0 copy-done.1
  89.6 0.6 copy.19
  90.2 0.0 copy-done
  90.2 0.8 copy.20
Async XLA Ops:
  86.8 2.7 %copy-start.1 = (f32[32,1,128]{2,1,0:T(1,128)S(1)}, f32[32,1,128]{2,1,0:T(1,128)}, u32[]{:S(2)}) copy-start(f32[32,1,128]{2,1,0:T(1,128)} %get-tuple-element.18) | copy-start | bytes 49156
  86.8 3.3 %copy-start = (f32[1024,128]{1,0:T(8,128)S(1)}, f32[1024,128]{1,0:T(8,128)}, u32[]{:S(2)}) copy-start(f32[1024,128]{1,0:T(8,128)} %get-tuple-element.11) | copy-start | bytes 1572868

commit v2 on v1

--- a/solution.py
+++ b/solution.py
@@ -77,9 +77,9 @@
     o_dens, o_vel, o_img, o_grad,
     ext, pack, xlo, xhi, pin, dens_k, ax_k, ay_k,
     rays, d_send, d_in, x_pieces, q_tab, spec, spec_end,
-    c_send, c_in, c_out, c_ret, p_spec, y_pieces, o_send, o_in,
+    c_send, c_in, c_out, c_ret, p_spec, y_pieces, o_send, o_in, h_send, h_in,
     prefix, w_light, v_light, gathered, rhs, sums, g_send, g_in,
-    halo_s, halo_r, dens_s, dens_r, d_s, d_r, c_s, c_r, b_s, b_r, o_s, o_r, g_s, g_r, tab_sem,
+    halo_s, halo_r, dens_s, dens_r, d_s, d_r, c_s, c_r, b_s, b_r, o_s, o_r, g_s, g_r, h_s, h_r, tab_sem,
 ):
     S, N, LX, K, VIEWS = sizes
     KP = K // N
@@ -94,6 +94,11 @@
 
     def penp(off):
         return lax.rem(pe + off + N, N)
+
+    def balanced(i, count):
+        odd = lax.rem(i, 2)
+        half = (i + 1) // 2
+        return odd * half + (1 - odd) * (count - half)
 
     table_copies = [pltpu.make_async_copy(tables_hbm.at[t], q_tab.at[t], tab_sem.at[t]) for t in range(3)]
     for copy in table_copies:
@@ -131,7 +136,7 @@
         return first, last
 
     nothing = jnp.zeros((K, LANES), f32)
-    first, last = lax.fori_loop(0, LX, pack_body, (nothing, nothing))
+    first, last = lax.fori_loop(0, LX, pack_body, (nothing, nothing), unroll=2)
     pack[0] = first
     pack[1] = last
     for field in range(4):
@@ -170,7 +175,7 @@
             ext[2, field, x + 1] = pltpu.roll(cells, LANES - 1, 1)
         return 0
 
-    lax.fori_loop(0, LX, spread_body, 0)
+    lax.fori_loop(0, LX, spread_body, 0, unroll=4)
     for copy in halo:
         copy.wait()
 
@@ -186,7 +191,7 @@
             ext[2, field, x + 1] = jnp.where(is_last, right, ext[2, field, x + 1])
         return 0
 
-    lax.fori_loop(0, LX, fix_body, 0)
+    lax.fori_loop(0, LX, fix_body, 0, unroll=4)
     for row, rows, slot, at in ((0, xlo, 0, LX - 1), (LX + 1, xhi, 2, 0)):
         for field in range(4):
             spot = field * LX + at
@@ -243,12 +248,12 @@
             b = dst.at[pl.ds(pl.multiple_of(start_at * src_rows, 8), src_rows)]
             return remote(a, b, s_sem.at[peer], r_sem.at[start_at], peer, pe)
 
-        def start():
-            def body(off, _):
-                descriptor(simp(off), me).start()
+        def start(first=1, end=S):
+            def body(i, _):
+                descriptor(simp(balanced(i, S)), me).start()
                 return 0
 
-            lax.fori_loop(1, S, body, 0)
+            lax.fori_loop(first, end, body, 0)
 
         def wait_recv():
             def body(off, _):
@@ -267,22 +272,34 @@
 
         return start, wait_recv, wait_send
 
+    half = N // 2
+    near_base = lax.div(pe, half) * half
+    far_base = half - near_base
+
     def pen_exchange(src, dst, s_sem, r_sem):
         def descriptor(peer, start_at):
             return remote(src.at[peer], dst.at[start_at], s_sem.at[peer], r_sem.at[start_at], me, peer)
 
+        def peer_of(i):
+            near = near_base + lax.rem(pe - near_base + 1 + i - half, half)
+            return jnp.where(i < half, far_base + i, near)
+
         def loop(method, swap):
-            def body(off, _):
-                peer = penp(off)
-                getattr(descriptor(peer, peer if swap else pe), method)()
-                return 0
-
-            lax.fori_loop(1, N, body, 0)
-
-        return (lambda: loop("start", False)), (lambda: loop("wait_recv", True)), (lambda: loop("wait_send", False))
+            def run(first=0, end=N - 1):
+                def body(i, _):
+                    peer = peer_of(i)
+                    getattr(descriptor(peer, peer if swap else pe), method)()
+                    return 0
+
+                lax.fori_loop(first, end, body, 0)
+
+            return run
+
+        return loop("start", False), loop("wait_recv", True), loop("wait_send", False)
 
     dens_x = sim_exchange(dens_k, LX, rays, dens_s, dens_r)
-    dens_x[0]()
+    early = S // 4
+    dens_x[0](1, early)
     mine = pl.ds(pl.multiple_of(me * LX, 8), LX)
     rays[mine, :] = dens_k[mine, :]
 
@@ -308,38 +325,63 @@
     lax.fori_loop(0, N, div_body, 0)
     d_x = pen_exchange(d_send, d_in, d_s, d_r)
     d_x[0]()
+    dens_x[0](early, S)
     d_in[pe] = d_send[pe]
     for copy in table_copies:
         copy.wait()
-    d_x[1]()
 
     lane_r = iota((ROWS, LANES), 1)
-    for part in range(N):
-        cells = d_in[part, 0:ROWS, :]
-        row = d_in[(part - 1) % N, ROWS + 8 : ROWS + 9, :]
-        column = jnp.transpose(jnp.broadcast_to(row, (LANES, ROWS)))
-        cells = cells - jnp.where(lane_r == 0, column, 0.0)
-        at = slice(part * LANES, (part + 1) * LANES)
-        high, low = split_two(cells)
-        x_pieces[0, 0:ROWS, at] = high
-        x_pieces[1, 0:ROWS, at] = low
-        high, low = split_two(d_in[part, ROWS:MSG, :])
-        x_pieces[0, ROWS:MSG, at] = high
-        x_pieces[1, ROWS:MSG, at] = low
-
-    wide = 2 * LANES
-
-    def forward_body(n, _):
-        at = pl.ds(pl.multiple_of(n * wide, wide), wide)
-        q0, q1 = q_tab[0, :, at], q_tab[1, :, at]
-        result = matmul(x_pieces[0], q0) + (matmul(x_pieces[0], q1) + matmul(x_pieces[1], q0))
-        for half in range(2):
-            columns = result[:, half * LANES : (half + 1) * LANES]
-            spec[pl.ds(pl.multiple_of((2 * n + half) * ROWS, 8), ROWS), :] = columns[0:ROWS]
-            spec_end[2 * n + half] = columns[ROWS : ROWS + 8]
-        return 0
-
-    lax.fori_loop(0, NY // wide, forward_body, 0)
+    WIDE = half * LANES
+
+    def column_fix(part):
+        row = d_in[part, ROWS + 8 : ROWS + 9, :]
+        return jnp.where(lane_r == 0, jnp.transpose(jnp.broadcast_to(row, (LANES, ROWS))), 0.0)
+
+    def stage(group, at, cells, end):
+        for t, piece in enumerate(split_two(cells)):
+            x_pieces[group, t * MSG : t * MSG + ROWS, at] = piece
+        for t, piece in enumerate(split_two(end)):
+            x_pieces[group, t * MSG + ROWS : (t + 1) * MSG, at] = piece
+
+    def stage_group(group, base):
+        for j in range(half):
+            cells = d_in[base + j, 0:ROWS, :]
+            if j > 0 or group == 1:
+                cells = cells - column_fix(lax.rem(base + j - 1 + N, N))
+            stage(group, slice(j * LANES, (j + 1) * LANES), cells, d_in[base + j, ROWS:MSG, :])
+
+    def transform(group, base, columns, part_rows):
+        wide = 2 * LANES
+        rows = pl.ds(pl.multiple_of(base * LANES, LANES), part_rows)
+
+        def body(n, _):
+            at = pl.ds(pl.multiple_of(n * wide, wide), wide)
+            both = matmul(x_pieces[group, :, columns], q_tab[0, rows, at])
+            high = matmul(x_pieces[group, 0:MSG, columns], q_tab[1, rows, at])
+            result = both[0:MSG] + (both[MSG : 2 * MSG] + high)
+            for side in range(2):
+                values = result[:, side * LANES : (side + 1) * LANES]
+                line = pl.ds(pl.multiple_of((2 * n + side) * ROWS, 8), ROWS)
+                if group == 0:
+                    spec[line, :] = values[0:ROWS]
+                    spec_end[2 * n + side] = values[ROWS : ROWS + 8]
+                else:
+                    spec[line, :] = spec[line, :] + values[0:ROWS]
+                    spec_end[2 * n + side] = spec_end[2 * n + side] + values[ROWS : ROWS + 8]
+            return 0
+
+        lax.fori_loop(0, NY // wide, body, 0)
+
+    d_x[1](half, N - 1)
+    stage_group(0, near_base)
+    transform(0, near_base, slice(0, WIDE), WIDE)
+    d_x[1](0, half)
+    stage_group(1, far_base)
+    stage(
+        1, slice(WIDE, WIDE + LANES), -column_fix(lax.rem(near_base - 1 + N, N)), jnp.zeros((MSG - ROWS, LANES), f32)
+    )
+    transform(1, far_base, slice(0, WIDE), WIDE)
+    transform(1, near_base, slice(WIDE, WIDE + LANES), LANES)
 
     LINES = N * KP
     root = lines[0]
@@ -549,7 +591,7 @@
 
     lax.fori_loop(0, SEG, grad_body, 0, unroll=4)
     g_x = sim_exchange(g_send, LX, g_in, g_s, g_r)
-    g_x[0]()
+    g_x[0](1, S // 2)
     g_in[mine, :] = g_send[mine, :]
 
     b_x[1]()
@@ -578,32 +620,43 @@
     for part in range(N):
         at = slice(part * LANES, (part + 1) * LANES)
         for t, piece in enumerate(split_three(p_spec[part * ROWS : (part + 1) * ROWS, :])):
-            y_pieces[t, 0:ROWS, at] = piece
+            y_pieces[t * MSG : t * MSG + ROWS, at] = piece
         end = jnp.concatenate([after[part * KP : (part + 1) * KP], jnp.zeros((MSG - ROWS - KP, LANES), f32)], axis=0)
         for t, piece in enumerate(split_three(end)):
-            y_pieces[t, ROWS:MSG, at] = piece
-
-    def inverse_body(n, _):
-        at = pl.ds(pl.multiple_of(n * wide, wide), wide)
-        q0, q1, q2 = q_tab[0, :, at], q_tab[1, :, at], q_tab[2, :, at]
-        y0, y1, y2 = y_pieces[0], y_pieces[1], y_pieces[2]
-        small = matmul(y1, q1) + matmul(y0, q2) + matmul(y2, q0)
-        result = matmul(y0, q0) + (matmul(y1, q0) + matmul(y0, q1) + small)
-        o_send[2 * n, :, :] = result[:, 0:LANES]
-        o_send[2 * n + 1, :, :] = result[:, LANES:wide]
-        return 0
-
-    lax.fori_loop(0, NY // wide, inverse_body, 0)
+            y_pieces[t * MSG + ROWS : (t + 1) * MSG, at] = piece
+
+    def inverse(base):
+        def body(n, _):
+            wide = PAIR * LANES
+            at = pl.ds(pl.multiple_of(base * LANES + n * wide, LANES), wide)
+            first = matmul(y_pieces[...], q_tab[0, :, at])
+            second = matmul(y_pieces[0 : 2 * MSG], q_tab[1, :, at])
+            third = matmul(y_pieces[0:MSG], q_tab[2, :, at])
+            small = second[MSG : 2 * MSG] + third + first[2 * MSG : 3 * MSG]
+            result = first[0:MSG] + (first[MSG : 2 * MSG] + second[0:MSG] + small)
+            for side in range(PAIR):
+                o_send[base + PAIR * n + side] = result[:, side * LANES : (side + 1) * LANES]
+            return 0
+
+        lax.fori_loop(0, half // PAIR, body, 0)
+
+    PAIR = min(2, half)
+    o_x = pen_exchange(o_send, o_in, o_s, o_r)
+    inverse(far_base)
+    o_x[0](0, half)
+    inverse(near_base)
+    o_x[0](half, N - 1)
     for part in range(N):
         turned = jnp.transpose(o_send[(part + 1) % N, 0:ROWS, :])
-        o_send[part, ROWS + 8 : ROWS + 16, :] = jnp.broadcast_to(turned[0:1, :], (8, ROWS))
-    o_x = pen_exchange(o_send, o_in, o_s, o_r)
-    o_x[0]()
+        h_send[part] = jnp.broadcast_to(turned[0:1, :], (8, ROWS))
+    h_x = pen_exchange(h_send, h_in, h_s, h_r)
+    h_x[0]()
+    g_x[0](S // 2, S)
     o_in[pe] = o_send[pe]
-    o_x[1]()
-
-    def velocity_body(part, _):
-        column = jnp.transpose(jnp.broadcast_to(o_in[part, ROWS + 8 : ROWS + 9, :], (LANES, ROWS)))
+    h_in[pe] = h_send[pe]
+
+    def velocity_part(part):
+        column = jnp.transpose(jnp.broadcast_to(h_in[part, 0:1, :], (LANES, ROWS)))
         for layer in range(KP):
             k = part * KP + layer
             at = pl.ds(pl.multiple_of(k * LX, 8), LX)
@@ -615,9 +668,20 @@
             )
             o_vel[pl.ds(k, LX, stride=K), :] = ax_k[at, :] - (next_x - here)
             o_vel[pl.ds(2 * LX * K + k, LX, stride=K), :] = ay_k[at, :] - (next_y - here)
-        return 0
-
-    lax.fori_loop(0, N, velocity_body, 0)
+
+    def velocity_group(base):
+        def body(j, _):
+            velocity_part(base + j)
+            return 0
+
+        lax.fori_loop(0, half, body, 0)
+
+    o_x[1](half, N - 1)
+    h_x[1](half, N - 1)
+    velocity_group(near_base)
+    o_x[1](0, half)
+    h_x[1](0, half)
+    velocity_group(far_base)
 
     g_x[1]()
 
@@ -626,8 +690,34 @@
         return 0
 
     lax.fori_loop(0, K, back_home, 0)
-    for copy_sends in (dens_x[2], d_x[2], c_x[2], b_x[2], g_x[2], o_x[2]):
+    for copy_sends in (dens_x[2], d_x[2], c_x[2], b_x[2], g_x[2], o_x[2], h_x[2]):
         copy_sends()
+
+
+def hand_over(*refs):
+    count = (len(refs) - 2) // 3
+    sources, targets, rooms = refs[:count], refs[count : 2 * count], refs[2 * count : 3 * count]
+    in_sem, out_sem = refs[3 * count :]
+    blocks = []
+    for source, target, room in zip(sources, targets, rooms):
+        rows = source.shape[0]
+        size = min(rows, 512)
+        for at in range(0, rows, size):
+            part = pl.ds(at, size)
+            slot = len(blocks)
+            blocks.append(
+                (
+                    pltpu.make_async_copy(source.at[part], room.at[part], in_sem.at[slot]),
+                    pltpu.make_async_copy(room.at[part], target.at[part], out_sem.at[slot]),
+                )
+            )
+    for fetch, _ in blocks:
+        fetch.start()
+    for fetch, store in blocks:
+        fetch.wait()
+        store.start()
+    for _, store in blocks:
+        store.wait()
 
 
 def solution(mesh):
@@ -654,7 +744,7 @@
             pltpu.VMEM((NX, LY), f32),
             pltpu.VMEM((N, MSG, LY), f32),
             pltpu.VMEM((N, MSG, LY), f32),
-            pltpu.VMEM((2, MSG, NY), bf16),
+            pltpu.VMEM((2, 2 * MSG, NY // 2 + LANES), bf16),
             pltpu.VMEM((3, NY, NY), bf16),
             pltpu.VMEM((N * 128, LANES), f32),
             pltpu.VMEM((N, 8, LANES), f32),
@@ -663,9 +753,11 @@
             pltpu.VMEM((S * 8, LANES), f32),
             pltpu.VMEM((S * 8, LANES), f32),
             pltpu.VMEM((N * 128, LANES), f32),
-            pltpu.VMEM((3, MSG, NY), bf16),
+            pltpu.VMEM((3 * MSG, NY), bf16),
             pltpu.VMEM((N, MSG, LY), f32),
             pltpu.VMEM((N, MSG, LY), f32),
+            pltpu.VMEM((N, 8, LY), f32),
+            pltpu.VMEM((N, 8, LY), f32),
             pltpu.VMEM((NX, LY), f32),
             pltpu.VMEM((NX, LY), f32),
             pltpu.VMEM((NX, LY), f32),
@@ -681,6 +773,7 @@
             dma((S,)), dma((S,)),
             dma((N,)), dma((N,)),
             dma((S,)), dma((S,)),
+            dma((N,)), dma((N,)),
             dma((3,)),
         ]
         density_new, velocity_new, images, gradient = pl.pallas_call(
@@ -698,6 +791,17 @@
                 collective_id=0, has_side_effects=True, vmem_limit_bytes=60 * 1024 * 1024
             ),
         )(density, velocity, stencil_code, fractions, targets, view_start, view_sign, tables, lines)
+        results = (density_new, velocity_new, images, gradient)
+        shapes = tuple(jax.ShapeDtypeStruct(value.shape, value.dtype) for value in results)
+        anywhere = pl.BlockSpec(memory_space=pl.ANY)
+        density_new, velocity_new, images, gradient = pl.pallas_call(
+            hand_over,
+            out_shape=shapes,
+            in_specs=[anywhere] * 4,
+            out_specs=(anywhere,) * 4,
+            scratch_shapes=[pltpu.VMEM(shape.shape, f32) for shape in shapes] + [dma((32,)), dma((32,))],
+            compiler_params=pltpu.CompilerParams(vmem_limit_bytes=60 * 1024 * 1024),
+        )(*results)
         return (
             density_new.reshape(LX, K, LY),
             velocity_new.reshape(3, LX, K, LY),

time: 91.1 us -> 85.3 us (0.936); the launches traced: 91 us -> 83.9 us
  local copies, waits for them, and re-layouts: 6 us -> 0 us
  Pallas kernels: 84.3 us -> 83.3 us
    unnamed x8 -> x0, local copies, waits for them, and re-layouts: 6 us -> none
    pallas_call x1, Pallas kernels: 84.3 us -> 80.3 us  [shards(): pl.pallas_call(functools.partial(step_kernel, (S, N, LX, K, VIEWS)), out_...]
    pallas_call x0 -> x1, Pallas kernels: none -> 3 us  [shards(): pl.pallas_call(hand_over, out_shape=shapes, in_specs=[anywhere] * 4, out_...]
where the time goes in v2:
time: 85.3 us; the launch traced here: 83.9 us
  Pallas kernels  83.3 us (98%)
    pallas_call x1, Pallas kernels, shards(): pl.pallas_call(functools.partial(step_kernel, (S, N, LX, K, VIEWS)), out_...  80.3 us
    pallas_call x1, Pallas kernels, shards(): pl.pallas_call(hand_over, out_shape=shapes, in_specs=[anywhere] * 4, out_...  3 us

profile of v2, /device:TPU:1, one launch (start us, length us, event | category | flops | bytes accessed | tf_op | source)
XLA Modules:
  0.0 83.9 jit_solution(14865831285088237069)
XLA Ops:
  0.6 80.3 %shard_map.120 = (f32[1024,128]{1,0:T(8,128)}, f32[3072,128]{1,0:T(8,128)}, f32[32,1,128]{2,1,0:T(1,128)}, f32[1024,128]{1,0:T(8,128)}) custom-call(f32[32,32,128]{2,1,0:T(8,128)} %dens.1, f32[3,32,32,128]{3,2,1,0:T(8,128)} %vel.1, s32[32,32,128]{2,1,0:T(8,128)} %code.1, f32[3,32,32,128]{3,2,1,0:T(8,128)} %frac.1, f32[32,1,128]{2,1,0:T(1,128)} %targ.1, ...), custom_call_target="tpu_custom_call" | custom-call | tf_op jit(solution)/shard_map/pallas_call | solution.py:779
  80.9 3.0 %shard_map.121 = (f32[1024,128]{1,0:T(8,128)}, f32[3072,128]{1,0:T(8,128)}, f32[32,1,128]{2,1,0:T(1,128)}, f32[1024,128]{1,0:T(8,128)}) custom-call(f32[1024,128]{1,0:T(8,128)} %get-tuple-element.12.refs_0_, f32[3072,128]{1,0:T(8,128)} %get-tuple-element.13.refs_1_, f32[32,1,128]{2,1,0:T(1,128)} %get-tuple-element.14.refs_2_, ...), custom_call_target="tpu_custom_call" | custom-call | tf_op jit(solution)/shard_map/pallas_call | solution.py:797

commit v3 on v2

--- a/solution.py
+++ b/solution.py
@@ -73,11 +73,12 @@
 
 def step_kernel(
     sizes,
-    dens, vel, code, frac, targ, vstart, vsign, tables_hbm, lines,
-    o_dens, o_vel, o_img, o_grad,
+    dens_hbm, vel_hbm, code_hbm, frac_hbm, targ, vstart, vsign, tables_hbm, lines,
+    o_dens_hbm, o_vel_hbm, o_img, o_grad_hbm,
+    dens, vel, code, frac, o_dens, o_vel, o_grad, io_sem,
     ext, pack, xlo, xhi, pin, dens_k, ax_k, ay_k,
     rays, d_send, d_in, x_pieces, q_tab, spec, spec_end,
-    c_send, c_in, c_out, c_ret, p_spec, y_pieces, o_send, o_in, h_send, h_in,
+    c_send, c_in, c_out, c_ret, ends, p_spec, y_pieces, o_send, o_in, h_send, h_in,
     prefix, w_light, v_light, gathered, rhs, sums, g_send, g_in,
     halo_s, halo_r, dens_s, dens_r, d_s, d_r, c_s, c_r, b_s, b_r, o_s, o_r, g_s, g_r, h_s, h_r, tab_sem,
 ):
@@ -100,6 +101,17 @@
         half = (i + 1) // 2
         return odd * half + (1 - odd) * (count - half)
 
+    parts = LX // 2
+    fields_in = [pltpu.make_async_copy(dens_hbm.at[pl.ds(h * parts, parts)], dens.at[pl.ds(h * parts, parts)], io_sem.at[h]) for h in range(2)]
+    fields_in += [
+        pltpu.make_async_copy(vel_hbm.at[c, pl.ds(h * parts, parts)], vel.at[c, pl.ds(h * parts, parts)], io_sem.at[2 + 2 * c + h])
+        for c in range(3)
+        for h in range(2)
+    ]
+    weights_in = [pltpu.make_async_copy(code_hbm, code, io_sem.at[8])]
+    weights_in += [pltpu.make_async_copy(frac_hbm.at[c], frac.at[c], io_sem.at[9 + c]) for c in range(3)]
+    for copy in fields_in + weights_in:
+        copy.start()
     table_copies = [pltpu.make_async_copy(tables_hbm.at[t], q_tab.at[t], tab_sem.at[t]) for t in range(3)]
     for copy in table_copies:
         copy.start()
@@ -119,6 +131,9 @@
     corners = ((-1, -1), (-1, 1), (1, -1), (1, 1))
     for dx, dy in corners:
         pl.semaphore_signal(barrier, inc=1, device_id={"sim": simp(dx), "pen": penp(dy)}, device_id_type=pl.DeviceIdType.MESH)
+
+    for copy in fields_in:
+        copy.wait()
 
     lane = iota((K, LANES), 1)
 
@@ -136,7 +151,7 @@
         return first, last
 
     nothing = jnp.zeros((K, LANES), f32)
-    first, last = lax.fori_loop(0, LX, pack_body, (nothing, nothing), unroll=2)
+    first, last = lax.fori_loop(0, LX, pack_body, (nothing, nothing), unroll=4)
     pack[0] = first
     pack[1] = last
     for field in range(4):
@@ -191,7 +206,7 @@
             ext[2, field, x + 1] = jnp.where(is_last, right, ext[2, field, x + 1])
         return 0
 
-    lax.fori_loop(0, LX, fix_body, 0, unroll=4)
+    lax.fori_loop(0, LX, fix_body, 0, unroll=8)
     for row, rows, slot, at in ((0, xlo, 0, LX - 1), (LX + 1, xhi, 2, 0)):
         for field in range(4):
             spot = field * LX + at
@@ -201,6 +216,9 @@
             ext[0, field, row] = jnp.where(is_first, left, pltpu.roll(cells, 1, 1))
             ext[1, field, row] = cells
             ext[2, field, row] = jnp.where(is_last, right, pltpu.roll(cells, LANES - 1, 1))
+
+    for copy in weights_in:
+        copy.wait()
 
     def weights(bit, fraction):
         rest = 1.0 - fraction
@@ -241,11 +259,21 @@
         return 0
 
     lax.fori_loop(0, LX, advect_body, 0)
+    block = LX * K
+    stores = [
+        pltpu.make_async_copy(o_dens, o_dens_hbm, io_sem.at[12]),
+        pltpu.make_async_copy(o_vel.at[pl.ds(block, block)], o_vel_hbm.at[pl.ds(block, block)], io_sem.at[13]),
+    ]
+    for copy in stores:
+        copy.start()
 
     def sim_exchange(src, src_rows, dst, s_sem, r_sem):
         def descriptor(peer, start_at):
-            a = src.at[pl.ds(pl.multiple_of(peer * src_rows, 8), src_rows)]
-            b = dst.at[pl.ds(pl.multiple_of(start_at * src_rows, 8), src_rows)]
+            if src_rows:
+                a = src.at[pl.ds(pl.multiple_of(peer * src_rows, 8), src_rows)]
+                b = dst.at[pl.ds(pl.multiple_of(start_at * src_rows, 8), src_rows)]
+            else:
+                a, b = src.at[peer], dst.at[start_at]
             return remote(a, b, s_sem.at[peer], r_sem.at[start_at], peer, pe)
 
         def start(first=1, end=S):
@@ -276,18 +304,18 @@
     near_base = lax.div(pe, half) * half
     far_base = half - near_base
 
+    def pen_peer(i):
+        near = near_base + lax.rem(pe - near_base + 1 + i, half)
+        return jnp.where(i < half, far_base + i, near)
+
     def pen_exchange(src, dst, s_sem, r_sem):
         def descriptor(peer, start_at):
             return remote(src.at[peer], dst.at[start_at], s_sem.at[peer], r_sem.at[start_at], me, peer)
 
-        def peer_of(i):
-            near = near_base + lax.rem(pe - near_base + 1 + i - half, half)
-            return jnp.where(i < half, far_base + i, near)
-
         def loop(method, swap):
             def run(first=0, end=N - 1):
                 def body(i, _):
-                    peer = peer_of(i)
+                    peer = pen_peer(i)
                     getattr(descriptor(peer, peer if swap else pe), method)()
                     return 0
 
@@ -306,7 +334,7 @@
     sub_x = iota((LX, LANES), 0)
     lane_x = iota((LX, LANES), 1)
 
-    def div_body(part, _):
+    def div_part(part):
         base = part * ROWS
         ends = []
         for layer in range(KP):
@@ -320,11 +348,16 @@
         d_send[part, ROWS : ROWS + 8, :] = jnp.concatenate(ends + [jnp.zeros((8 - KP, LANES), f32)], axis=0)
         turned = jnp.transpose(ay_k[pl.ds(pl.multiple_of(base, 8), ROWS), :])
         d_send[part, ROWS + 8 : ROWS + 16, :] = jnp.broadcast_to(turned[LANES - 1 : LANES, :], (8, ROWS))
-        return 0
-
-    lax.fori_loop(0, N, div_body, 0)
+
     d_x = pen_exchange(d_send, d_in, d_s, d_r)
-    d_x[0]()
+
+    def div_send(i, _):
+        div_part(pen_peer(i))
+        d_x[0](i, i + 1)
+        return 0
+
+    lax.fori_loop(0, N - 1, div_send, 0)
+    div_part(pe)
     dens_x[0](early, S)
     d_in[pe] = d_send[pe]
     for copy in table_copies:
@@ -402,18 +435,14 @@
     fwd, bwd, acc = lax.fori_loop(0, LX, ends_body, (flat, root * beyond, flat), unroll=2)
     fwd = fwd + root_inv * beyond
 
-    def carry_row(row):
-        return pl.ds(row, LINES, stride=8)
-
-    c_send[carry_row(0), :] = fwd
-    c_send[carry_row(1), :] = bwd
-    c_send[carry_row(2), :] = acc
-    for row in range(3, 8):
-        c_send[carry_row(row), :] = flat
-    c_x = sim_exchange(c_send, 8, c_in, c_s, c_r)
+    alone = jnp.logical_and(iota((LINES, LANES), 1) == 0, iota((LINES, LANES), 0) < KP)
+    bwd = jnp.where(alone, acc, bwd)
+    for line in range(LINES):
+        c_send[line, 0:1, :] = fwd[line : line + 1]
+        c_send[line, 1:2, :] = bwd[line : line + 1]
+    c_x = sim_exchange(c_send, 0, c_in, c_s, c_r)
     c_x[0]()
-    my_carry = pl.ds(pl.multiple_of(me * 8, 8), 8)
-    c_in[my_carry, :] = c_send[my_carry, :]
+    c_in[me] = c_send[me]
 
     dens_x[1]()
 
@@ -475,17 +504,14 @@
     lax.fori_loop(0, SEG, finish_body, 0, unroll=4)
 
     c_x[1]()
-    block = lines[4, pl.ds(me, 1), :]
+    power = lines[4, pl.ds(me, 1), :]
     close = lines[5, pl.ds(me, 1), :]
     lone = jnp.logical_and(iota((1, LANES), 1) == 0, me < KP)
 
-    def carry_at(i, row):
-        return pl.ds(8 * i + row, 1)
-
     def around_body(i, carry):
         a, b = carry
-        a = c_in[carry_at(i, 0), :] + block * a
-        b = c_in[carry_at(S - 1 - i, 1), :] + block * b
+        a = c_in[i, 0:1, :] + power * a
+        b = c_in[S - 1 - i, 1:2, :] + power * b
         return a, b
 
     a, b = lax.fori_loop(0, S, around_body, (one, one))
@@ -493,26 +519,24 @@
     def carry_body(i, carry):
         a, b, total = carry
         j = S - 1 - i
-        c_out[carry_at(i, 0), :] = a
-        c_out[carry_at(j, 1), :] = b
-        total = total + (c_in[carry_at(i, 2), :] + LX * a)
-        return c_in[carry_at(i, 0), :] + block * a, c_in[carry_at(j, 1), :] + block * b, total
+        c_out[i, 0:1, :] = a
+        c_out[j, 1:2, :] = b
+        total = total + (c_in[i, 1:2, :] + LX * a)
+        return c_in[i, 0:1, :] + power * a, c_in[j, 1:2, :] + power * b, total
 
     _, _, total = lax.fori_loop(0, S, carry_body, (a * close, b * close, one))
     mean = total * (1.0 / NX)
 
     def lone_body(i, offset):
-        slope = c_out[carry_at(i, 0), :] - mean
-        c_out[carry_at(i, 0), :] = jnp.where(lone, slope, c_out[carry_at(i, 0), :])
-        c_out[carry_at(i, 1), :] = jnp.where(lone, offset, c_out[carry_at(i, 1), :])
-        return offset + (c_in[carry_at(i, 2), :] + LX * slope)
+        slope = c_out[i, 0:1, :] - mean
+        c_out[i, 0:1, :] = jnp.where(lone, slope, c_out[i, 0:1, :])
+        c_out[i, 1:2, :] = jnp.where(lone, offset, c_out[i, 1:2, :])
+        return offset + (c_in[i, 1:2, :] + LX * slope)
 
     lax.fori_loop(0, S, lone_body, one)
-    for row in range(2, 8):
-        c_out[carry_row(row), :] = flat
-    b_x = sim_exchange(c_out, 8, c_ret, b_s, b_r)
+    b_x = sim_exchange(c_out, 0, c_ret, b_s, b_r)
     b_x[0]()
-    c_ret[my_carry, :] = c_out[my_carry, :]
+    c_ret[me] = c_out[me]
 
     sub_v = iota((VIEWS, LANES), 0)
     lane_m = iota((1, 6 * VIEWS), 1)
@@ -597,9 +621,11 @@
     b_x[1]()
     factor_f = lines[2]
     factor_b = lines[3]
-    alone = jnp.logical_and(iota((LINES, LANES), 1) == 0, iota((LINES, LANES), 0) < KP)
-    first_f = c_ret[carry_row(0), :]
-    tail = c_ret[carry_row(1), :]
+    for line in range(LINES):
+        ends[0, line : line + 1, :] = c_ret[line, 0:1, :]
+        ends[1, line : line + 1, :] = c_ret[line, 1:2, :]
+    first_f = ends[0]
+    tail = ends[1]
     back_in = tail + root * beyond
 
     def back_body(i, bwd):
@@ -683,13 +709,27 @@
     h_x[1](0, half)
     velocity_group(far_base)
 
+    late = [
+        pltpu.make_async_copy(o_vel.at[pl.ds(at, block // 2)], o_vel_hbm.at[pl.ds(at, block // 2)], io_sem.at[slot])
+        for slot, at in ((14, 0), (15, block // 2), (16, 2 * block), (17, 2 * block + block // 2))
+    ]
+    for copy in late:
+        copy.start()
     g_x[1]()
 
     def back_home(k, _):
         o_grad[pl.ds(k, LX, stride=K), :] = g_in[pl.ds(pl.multiple_of(k * LX, 8), LX), :]
         return 0
 
-    lax.fori_loop(0, K, back_home, 0)
+    lax.fori_loop(0, K, back_home, 0, unroll=4)
+    late += [
+        pltpu.make_async_copy(o_grad.at[pl.ds(at, block // 2)], o_grad_hbm.at[pl.ds(at, block // 2)], io_sem.at[slot])
+        for slot, at in ((18, 0), (19, block // 2))
+    ]
+    for copy in late[4:]:
+        copy.start()
+    for copy in stores + late:
+        copy.wait()
     for copy_sends in (dens_x[2], d_x[2], c_x[2], b_x[2], g_x[2], o_x[2], h_x[2]):
         copy_sends()
 
@@ -729,10 +769,19 @@
         NX, NY = LX * S, LY * N
         tables = jnp.asarray(hartley_pieces(NY))
         lines = jnp.asarray(line_tables(NY, NX, LX, K // N))
+        anywhere = pl.BlockSpec(memory_space=pl.ANY)
         vmem = pl.BlockSpec(memory_space=pltpu.VMEM)
         smem = pl.BlockSpec(memory_space=pltpu.SMEM)
         dma = pltpu.SemaphoreType.DMA
         scratch = [
+            pltpu.VMEM((LX, K, LY), f32),
+            pltpu.VMEM((3, LX, K, LY), f32),
+            pltpu.VMEM((LX, K, LY), jnp.int32),
+            pltpu.VMEM((3, LX, K, LY), f32),
+            pltpu.VMEM((LX * K, LY), f32),
+            pltpu.VMEM((3 * LX * K, LY), f32),
+            pltpu.VMEM((LX * K, LY), f32),
+            dma((20,)),
             pltpu.VMEM((3, 4, LX + 2, K, LY), f32),
             pltpu.VMEM((10, K, LY), f32),
             pltpu.VMEM((4, K, LY), f32),
@@ -748,10 +797,11 @@
             pltpu.VMEM((3, NY, NY), bf16),
             pltpu.VMEM((N * 128, LANES), f32),
             pltpu.VMEM((N, 8, LANES), f32),
-            pltpu.VMEM((S * 8, LANES), f32),
-            pltpu.VMEM((S * 8, LANES), f32),
-            pltpu.VMEM((S * 8, LANES), f32),
-            pltpu.VMEM((S * 8, LANES), f32),
+            pltpu.VMEM((S, 2, LANES), f32),
+            pltpu.VMEM((S, 2, LANES), f32),
+            pltpu.VMEM((S, 2, LANES), f32),
+            pltpu.VMEM((S, 2, LANES), f32),
+            pltpu.VMEM((2, S, LANES), f32),
             pltpu.VMEM((N * 128, LANES), f32),
             pltpu.VMEM((3 * MSG, NY), bf16),
             pltpu.VMEM((N, MSG, LY), f32),
@@ -784,8 +834,8 @@
                 jax.ShapeDtypeStruct(targets.shape, f32),
                 jax.ShapeDtypeStruct((LX * K, LY), f32),
             ),
-            in_specs=[vmem, vmem, vmem, vmem, vmem, smem, smem, pl.BlockSpec(memory_space=pl.ANY), vmem],
-            out_specs=(vmem, vmem, vmem, vmem),
+            in_specs=[anywhere] * 4 + [vmem, smem, smem, anywhere, vmem],
+            out_specs=(anywhere, anywhere, vmem, anywhere),
             scratch_shapes=scratch,
             compiler_params=pltpu.CompilerParams(
                 collective_id=0, has_side_effects=True, vmem_limit_bytes=60 * 1024 * 1024
@@ -793,7 +843,6 @@
         )(density, velocity, stencil_code, fractions, targets, view_start, view_sign, tables, lines)
         results = (density_new, velocity_new, images, gradient)
         shapes = tuple(jax.ShapeDtypeStruct(value.shape, value.dtype) for value in results)
-        anywhere = pl.BlockSpec(memory_space=pl.ANY)
         density_new, velocity_new, images, gradient = pl.pallas_call(
             hand_over,
             out_shape=shapes,

time: 85.3 us -> 80.6 us (0.945); the launches traced: 83.9 us -> 80.5 us
  Pallas kernels: 83.3 us -> 79.8 us
    pallas_call x1, Pallas kernels: 80.3 us -> 76.8 us  [shards(): pl.pallas_call(functools.partial(step_kernel, (S, N, LX, K, VIEWS)), out_...]
where the time goes in v3:
time: 80.6 us; the launch traced here: 80.5 us
  Pallas kernels  79.8 us (99%)
    pallas_call x1, Pallas kernels, shards(): pl.pallas_call(functools.partial(step_kernel, (S, N, LX, K, VIEWS)), out_...  76.8 us
    pallas_call x1, Pallas kernels, shards(): pl.pallas_call(hand_over, out_shape=shapes, in_specs=[anywhere] * 4, out_...  3 us

profile of v3, /device:TPU:1, one launch (start us, length us, event | category | flops | bytes accessed | tf_op | source)
XLA Modules:
  0.0 80.5 jit_solution(14374696367292505075)
XLA Ops:
  0.6 76.8 %shard_map.120 = (f32[1024,128]{1,0:T(8,128)}, f32[3072,128]{1,0:T(8,128)}, f32[32,1,128]{2,1,0:T(1,128)}, f32[1024,128]{1,0:T(8,128)}) custom-call(f32[32,32,128]{2,1,0:T(8,128)} %dens_hbm.1, f32[3,32,32,128]{3,2,1,0:T(8,128)} %vel_hbm.1, s32[32,32,128]{2,1,0:T(8,128)} %code_hbm.1, f32[3,32,32,128]{3,2,1,0:T(8,128)} %frac_hbm.1, f32[32,1,128]{2,1,0:T(1,128)} %targ.1, ...), custom_call_target="tpu_custom_call" | custom-call | tf_op jit(solution)/shard_map/pallas_call | solution.py:829
  77.5 3.0 %shard_map.121 = (f32[1024,128]{1,0:T(8,128)}, f32[3072,128]{1,0:T(8,128)}, f32[32,1,128]{2,1,0:T(1,128)}, f32[1024,128]{1,0:T(8,128)}) custom-call(f32[1024,128]{1,0:T(8,128)} %get-tuple-element.12.refs_0_, f32[3072,128]{1,0:T(8,128)} %get-tuple-element.13.refs_1_, f32[32,1,128]{2,1,0:T(1,128)} %get-tuple-element.14.refs_2_, ...), custom_call_target="tpu_custom_call" | custom-call | tf_op jit(solution)/shard_map/pallas_call | solution.py:846

commit v4 on v3

--- a/solution.py
+++ b/solution.py
@@ -73,12 +73,12 @@
 
 def step_kernel(
     sizes,
-    dens_hbm, vel_hbm, code_hbm, frac_hbm, targ, vstart, vsign, tables_hbm, lines,
+    dens_hbm, vel_hbm, code_hbm, frac_hbm, targ, vstart, vsign, tables_hbm, lines, q_first,
     o_dens_hbm, o_vel_hbm, o_img, o_grad_hbm,
     dens, vel, code, frac, o_dens, o_vel, o_grad, io_sem,
     ext, pack, xlo, xhi, pin, dens_k, ax_k, ay_k,
     rays, d_send, d_in, x_pieces, q_tab, spec, spec_end,
-    c_send, c_in, c_out, c_ret, ends, p_spec, y_pieces, o_send, o_in, h_send, h_in,
+    c_send, c_in, c_out, c_ret, ends, p_spec, y_pieces, o_send, o_in, h_send, h_in, h_columns,
     prefix, w_light, v_light, gathered, rhs, sums, g_send, g_in,
     halo_s, halo_r, dens_s, dens_r, d_s, d_r, c_s, c_r, b_s, b_r, o_s, o_r, g_s, g_r, h_s, h_r, tab_sem,
 ):
@@ -86,6 +86,7 @@
     KP = K // N
     NX, NY = S * LX, N * LANES
     ROWS = KP * LX
+    SENT = ROWS + 8
     SEG = NX // SEGMENTS
     me = lax.axis_index("sim")
     pe = lax.axis_index("pen")
@@ -298,7 +299,11 @@
 
             lax.fori_loop(1, S, body, 0)
 
-        return start, wait_recv, wait_send
+        def wait_one(i):
+            peer = simp(balanced(i, S))
+            descriptor(peer, peer).wait_recv()
+
+        return start, wait_recv, wait_send, wait_one
 
     half = N // 2
     near_base = lax.div(pe, half) * half
@@ -345,9 +350,9 @@
             before_y = jnp.where(lane_x == 0, 0.0, pltpu.roll(ay, 1, 1))
             d_send[part, layer * LX : (layer + 1) * LX, :] = (ax - before_x) + (ay - before_y)
             ends.append(-ax[LX - 1 : LX, :])
-        d_send[part, ROWS : ROWS + 8, :] = jnp.concatenate(ends + [jnp.zeros((8 - KP, LANES), f32)], axis=0)
         turned = jnp.transpose(ay_k[pl.ds(pl.multiple_of(base, 8), ROWS), :])
-        d_send[part, ROWS + 8 : ROWS + 16, :] = jnp.broadcast_to(turned[LANES - 1 : LANES, :], (8, ROWS))
+        ends.append(turned[LANES - 1 : LANES, :])
+        d_send[part, ROWS:SENT, :] = jnp.concatenate(ends + [jnp.zeros((7 - KP, LANES), f32)], axis=0)
 
     d_x = pen_exchange(d_send, d_in, d_s, d_r)
 
@@ -363,12 +368,7 @@
     for copy in table_copies:
         copy.wait()
 
-    lane_r = iota((ROWS, LANES), 1)
     WIDE = half * LANES
-
-    def column_fix(part):
-        row = d_in[part, ROWS + 8 : ROWS + 9, :]
-        return jnp.where(lane_r == 0, jnp.transpose(jnp.broadcast_to(row, (LANES, ROWS))), 0.0)
 
     def stage(group, at, cells, end):
         for t, piece in enumerate(split_two(cells)):
@@ -379,18 +379,16 @@
     def stage_group(group, base):
         for j in range(half):
             cells = d_in[base + j, 0:ROWS, :]
-            if j > 0 or group == 1:
-                cells = cells - column_fix(lax.rem(base + j - 1 + N, N))
-            stage(group, slice(j * LANES, (j + 1) * LANES), cells, d_in[base + j, ROWS:MSG, :])
-
-    def transform(group, base, columns, part_rows):
+            end = jnp.concatenate([d_in[base + j, ROWS : ROWS + KP, :], jnp.zeros((MSG - ROWS - KP, LANES), f32)], axis=0)
+            stage(group, slice(j * LANES, (j + 1) * LANES), cells, end)
+
+    def transform(group, table, rows, columns):
         wide = 2 * LANES
-        rows = pl.ds(pl.multiple_of(base * LANES, LANES), part_rows)
 
         def body(n, _):
             at = pl.ds(pl.multiple_of(n * wide, wide), wide)
-            both = matmul(x_pieces[group, :, columns], q_tab[0, rows, at])
-            high = matmul(x_pieces[group, 0:MSG, columns], q_tab[1, rows, at])
+            both = matmul(x_pieces[group, :, columns], table[0, rows, at])
+            high = matmul(x_pieces[group, 0:MSG, columns], table[1, rows, at])
             result = both[0:MSG] + (both[MSG : 2 * MSG] + high)
             for side in range(2):
                 values = result[:, side * LANES : (side + 1) * LANES]
@@ -407,14 +405,15 @@
 
     d_x[1](half, N - 1)
     stage_group(0, near_base)
-    transform(0, near_base, slice(0, WIDE), WIDE)
+    transform(0, q_tab, pl.ds(pl.multiple_of(near_base * LANES, LANES), WIDE), slice(0, WIDE))
     d_x[1](0, half)
     stage_group(1, far_base)
-    stage(
-        1, slice(WIDE, WIDE + LANES), -column_fix(lax.rem(near_base - 1 + N, N)), jnp.zeros((MSG - ROWS, LANES), f32)
+    ahead = jnp.concatenate(
+        [d_in[part, ROWS + KP : ROWS + KP + 1, :] for part in range(N)] + [jnp.zeros((LANES - N, ROWS), f32)], axis=0
     )
-    transform(1, far_base, slice(0, WIDE), WIDE)
-    transform(1, near_base, slice(WIDE, WIDE + LANES), LANES)
+    stage(1, slice(WIDE, WIDE + LANES), -jnp.transpose(ahead), jnp.zeros((MSG - ROWS, LANES), f32))
+    transform(1, q_tab, pl.ds(pl.multiple_of(far_base * LANES, LANES), WIDE), slice(0, WIDE))
+    transform(1, q_first, slice(0, LANES), slice(WIDE, WIDE + LANES))
 
     LINES = N * KP
     root = lines[0]
@@ -432,7 +431,7 @@
         bwd = root * (spec[at_x(LX - 1 - i), :] + bwd)
         return fwd, bwd, acc
 
-    fwd, bwd, acc = lax.fori_loop(0, LX, ends_body, (flat, root * beyond, flat), unroll=2)
+    fwd, bwd, acc = lax.fori_loop(0, LX, ends_body, (flat, root * beyond, flat), unroll=4)
     fwd = fwd + root_inv * beyond
 
     alone = jnp.logical_and(iota((LINES, LANES), 1) == 0, iota((LINES, LANES), 0) < KP)
@@ -514,7 +513,7 @@
         b = c_in[S - 1 - i, 1:2, :] + power * b
         return a, b
 
-    a, b = lax.fori_loop(0, S, around_body, (one, one))
+    a, b = lax.fori_loop(0, S, around_body, (one, one), unroll=8)
 
     def carry_body(i, carry):
         a, b, total = carry
@@ -524,7 +523,7 @@
         total = total + (c_in[i, 1:2, :] + LX * a)
         return c_in[i, 0:1, :] + power * a, c_in[j, 1:2, :] + power * b, total
 
-    _, _, total = lax.fori_loop(0, S, carry_body, (a * close, b * close, one))
+    _, _, total = lax.fori_loop(0, S, carry_body, (a * close, b * close, one), unroll=8)
     mean = total * (1.0 / NX)
 
     def lone_body(i, offset):
@@ -533,7 +532,7 @@
         c_out[i, 1:2, :] = jnp.where(lone, offset, c_out[i, 1:2, :])
         return offset + (c_in[i, 1:2, :] + LX * slope)
 
-    lax.fori_loop(0, S, lone_body, one)
+    lax.fori_loop(0, S, lone_body, one, unroll=8)
     b_x = sim_exchange(c_out, 0, c_ret, b_s, b_r)
     b_x[0]()
     c_ret[me] = c_out[me]
@@ -633,7 +632,7 @@
         p_spec[at_x(x), :] = factor_b * bwd
         return root * (spec[at_x(x), :] + bwd)
 
-    lax.fori_loop(0, LX, back_body, back_in, unroll=2)
+    lax.fori_loop(0, LX, back_body, back_in, unroll=4)
 
     def front_body(x, carry):
         fwd, height = carry
@@ -641,7 +640,7 @@
         p_spec[at_x(x), :] = p_spec[at_x(x), :] + factor_f * jnp.where(alone, height, fwd)
         return fwd, height + fwd
 
-    fwd, height = lax.fori_loop(0, LX, front_body, (first_f, tail), unroll=2)
+    fwd, height = lax.fori_loop(0, LX, front_body, (first_f, tail), unroll=4)
     after = factor_f * jnp.where(alone, height, root * fwd) + factor_b * (root_inv * back_in)
     for part in range(N):
         at = slice(part * LANES, (part + 1) * LANES)
@@ -651,7 +650,7 @@
         for t, piece in enumerate(split_three(end)):
             y_pieces[t * MSG + ROWS : (t + 1) * MSG, at] = piece
 
-    def inverse(base):
+    def inverse(base, far):
         def body(n, _):
             wide = PAIR * LANES
             at = pl.ds(pl.multiple_of(base * LANES + n * wide, LANES), wide)
@@ -661,16 +660,17 @@
             small = second[MSG : 2 * MSG] + third + first[2 * MSG : 3 * MSG]
             result = first[0:MSG] + (first[MSG : 2 * MSG] + second[0:MSG] + small)
             for side in range(PAIR):
-                o_send[base + PAIR * n + side] = result[:, side * LANES : (side + 1) * LANES]
+                o_send[base + PAIR * n + side] = result[0:SENT, side * LANES : (side + 1) * LANES]
+            if far:
+                o_x[0](PAIR * n, PAIR * (n + 1))
             return 0
 
         lax.fori_loop(0, half // PAIR, body, 0)
 
     PAIR = min(2, half)
     o_x = pen_exchange(o_send, o_in, o_s, o_r)
-    inverse(far_base)
-    o_x[0](0, half)
-    inverse(near_base)
+    inverse(far_base, True)
+    inverse(near_base, False)
     o_x[0](half, N - 1)
     for part in range(N):
         turned = jnp.transpose(o_send[(part + 1) % N, 0:ROWS, :])
@@ -682,7 +682,7 @@
     h_in[pe] = h_send[pe]
 
     def velocity_part(part):
-        column = jnp.transpose(jnp.broadcast_to(h_in[part, 0:1, :], (LANES, ROWS)))
+        column = pltpu.roll(h_columns[...], LANES - 1 - part, 1)
         for layer in range(KP):
             k = part * KP + layer
             at = pl.ds(pl.multiple_of(k * LX, 8), LX)
@@ -702,12 +702,29 @@
 
         lax.fori_loop(0, half, body, 0)
 
+    h_x[1]()
+    heads = jnp.concatenate([h_in[part, 0:1, :] for part in range(N)] + [jnp.zeros((LANES - N, ROWS), f32)], axis=0)
+    h_columns[...] = jnp.transpose(heads)
     o_x[1](half, N - 1)
-    h_x[1](half, N - 1)
     velocity_group(near_base)
-    o_x[1](0, half)
-    h_x[1](0, half)
-    velocity_group(far_base)
+
+    def back_home(k):
+        o_grad[pl.ds(k, LX, stride=K), :] = g_in[pl.ds(pl.multiple_of(k * LX, 8), LX), :]
+
+    def bring_home(i, _):
+        g_x[3](i)
+        back_home(simp(balanced(i, S)))
+        return 0
+
+    back_home(me)
+    lax.fori_loop(1, S // 2, bring_home, 0)
+
+    def far_velocity(i, _):
+        o_x[1](i, i + 1)
+        velocity_part(far_base + i)
+        return 0
+
+    lax.fori_loop(0, half, far_velocity, 0)
 
     late = [
         pltpu.make_async_copy(o_vel.at[pl.ds(at, block // 2)], o_vel_hbm.at[pl.ds(at, block // 2)], io_sem.at[slot])
@@ -715,13 +732,7 @@
     ]
     for copy in late:
         copy.start()
-    g_x[1]()
-
-    def back_home(k, _):
-        o_grad[pl.ds(k, LX, stride=K), :] = g_in[pl.ds(pl.multiple_of(k * LX, 8), LX), :]
-        return 0
-
-    lax.fori_loop(0, K, back_home, 0, unroll=4)
+    lax.fori_loop(S // 2, S, bring_home, 0)
     late += [
         pltpu.make_async_copy(o_grad.at[pl.ds(at, block // 2)], o_grad_hbm.at[pl.ds(at, block // 2)], io_sem.at[slot])
         for slot, at in ((18, 0), (19, block // 2))
@@ -767,7 +778,10 @@
         LX, K, LY = density.shape
         VIEWS = targets.shape[0]
         NX, NY = LX * S, LY * N
-        tables = jnp.asarray(hartley_pieces(NY))
+        pieces = hartley_pieces(NY)
+        tables = jnp.asarray(pieces)
+        chosen = pieces[0:2, (np.arange(1, N + 1) * LY) % NY]
+        firsts = jnp.asarray(np.concatenate([chosen, np.zeros((2, LANES - N, NY), chosen.dtype)], axis=1))
         lines = jnp.asarray(line_tables(NY, NX, LX, K // N))
         anywhere = pl.BlockSpec(memory_space=pl.ANY)
         vmem = pl.BlockSpec(memory_space=pltpu.VMEM)
@@ -791,8 +805,8 @@
             pltpu.VMEM((K * LX, LY), f32),
             pltpu.VMEM((K * LX, LY), f32),
             pltpu.VMEM((NX, LY), f32),
-            pltpu.VMEM((N, MSG, LY), f32),
-            pltpu.VMEM((N, MSG, LY), f32),
+            pltpu.VMEM((N, 136, LY), f32),
+            pltpu.VMEM((N, 136, LY), f32),
             pltpu.VMEM((2, 2 * MSG, NY // 2 + LANES), bf16),
             pltpu.VMEM((3, NY, NY), bf16),
             pltpu.VMEM((N * 128, LANES), f32),
@@ -804,10 +818,11 @@
             pltpu.VMEM((2, S, LANES), f32),
             pltpu.VMEM((N * 128, LANES), f32),
             pltpu.VMEM((3 * MSG, NY), bf16),
-            pltpu.VMEM((N, MSG, LY), f32),
-            pltpu.VMEM((N, MSG, LY), f32),
+            pltpu.VMEM((N, 136, LY), f32),
+            pltpu.VMEM((N, 136, LY), f32),
             pltpu.VMEM((N, 8, LY), f32),
             pltpu.VMEM((N, 8, LY), f32),
+            pltpu.VMEM((128, LANES), f32),
             pltpu.VMEM((NX, LY), f32),
             pltpu.VMEM((NX, LY), f32),
             pltpu.VMEM((NX, LY), f32),
@@ -834,13 +849,13 @@
                 jax.ShapeDtypeStruct(targets.shape, f32),
                 jax.ShapeDtypeStruct((LX * K, LY), f32),
             ),
-            in_specs=[anywhere] * 4 + [vmem, smem, smem, anywhere, vmem],
+            in_specs=[anywhere] * 4 + [vmem, smem, smem, anywhere, vmem, vmem],
             out_specs=(anywhere, anywhere, vmem, anywhere),
             scratch_shapes=scratch,
             compiler_params=pltpu.CompilerParams(
                 collective_id=0, has_side_effects=True, vmem_limit_bytes=60 * 1024 * 1024
             ),
-        )(density, velocity, stencil_code, fractions, targets, view_start, view_sign, tables, lines)
+        )(density, velocity, stencil_code, fractions, targets, view_start, view_sign, tables, lines, firsts)
         results = (density_new, velocity_new, images, gradient)
         shapes = tuple(jax.ShapeDtypeStruct(value.shape, value.dtype) for value in results)
         density_new, velocity_new, images, gradient = pl.pallas_call(

time: 80.6 us -> 79.1 us (0.981)
  Pallas kernels: 79.8 us -> 78.2 us
    pallas_call x1, Pallas kernels: 76.8 us -> 75.2 us  [shards(): pl.pallas_call(functools.partial(step_kernel, (S, N, LX, K, VIEWS)), out_...]
where the time goes in v4:
time: 79.1 us; the launch traced here: 78.8 us
  Pallas kernels  78.2 us (99%)
    pallas_call x1, Pallas kernels, shards(): pl.pallas_call(functools.partial(step_kernel, (S, N, LX, K, VIEWS)), out_...  75.2 us
    pallas_call x1, Pallas kernels, shards(): pl.pallas_call(hand_over, out_shape=shapes, in_specs=[anywhere] * 4, out_...  3 us

profile of v4, /device:TPU:1, one launch (start us, length us, event | category | flops | bytes accessed | tf_op | source)
XLA Modules:
  0.0 78.8 jit_solution(11625620383471332687)
XLA Ops:
  0.6 75.2 %shard_map.129 = (f32[1024,128]{1,0:T(8,128)}, f32[3072,128]{1,0:T(8,128)}, f32[32,1,128]{2,1,0:T(1,128)}, f32[1024,128]{1,0:T(8,128)}) custom-call(f32[32,32,128]{2,1,0:T(8,128)} %dens_hbm.1, f32[3,32,32,128]{3,2,1,0:T(8,128)} %vel_hbm.1, s32[32,32,128]{2,1,0:T(8,128)} %code_hbm.1, f32[3,32,32,128]{3,2,1,0:T(8,128)} %frac_hbm.1, f32[32,1,128]{2,1,0:T(1,128)} %targ.1, ...), custom_call_target="tpu_custom_call" | custom-call | tf_op jit(solution)/shard_map/pallas_call | solution.py:844
  75.8 3.0 %shard_map.130 = (f32[1024,128]{1,0:T(8,128)}, f32[3072,128]{1,0:T(8,128)}, f32[32,1,128]{2,1,0:T(1,128)}, f32[1024,128]{1,0:T(8,128)}) custom-call(f32[1024,128]{1,0:T(8,128)} %get-tuple-element.12.refs_0_, f32[3072,128]{1,0:T(8,128)} %get-tuple-element.13.refs_1_, f32[32,1,128]{2,1,0:T(1,128)} %get-tuple-element.14.refs_2_, ...), custom_call_target="tpu_custom_call" | custom-call | tf_op jit(solution)/shard_map/pallas_call | solution.py:861

commit v5 on v4

--- a/solution.py
+++ b/solution.py
@@ -111,11 +111,9 @@
     ]
     weights_in = [pltpu.make_async_copy(code_hbm, code, io_sem.at[8])]
     weights_in += [pltpu.make_async_copy(frac_hbm.at[c], frac.at[c], io_sem.at[9 + c]) for c in range(3)]
-    for copy in fields_in + weights_in:
+    for copy in fields_in:
         copy.start()
     table_copies = [pltpu.make_async_copy(tables_hbm.at[t], q_tab.at[t], tab_sem.at[t]) for t in range(3)]
-    for copy in table_copies:
-        copy.start()
 
     barrier = pltpu.get_barrier_semaphore()
 
@@ -135,6 +133,8 @@
 
     for copy in fields_in:
         copy.wait()
+    for copy in weights_in:
+        copy.start()
 
     lane = iota((K, LANES), 1)
 
@@ -152,7 +152,7 @@
         return first, last
 
     nothing = jnp.zeros((K, LANES), f32)
-    first, last = lax.fori_loop(0, LX, pack_body, (nothing, nothing), unroll=4)
+    first, last = lax.fori_loop(0, LX, pack_body, (nothing, nothing), unroll=16)
     pack[0] = first
     pack[1] = last
     for field in range(4):
@@ -182,6 +182,8 @@
             )
     for copy in halo:
         copy.start()
+    for copy in table_copies:
+        copy.start()
 
     def spread_body(x, _):
         for field in range(4):
@@ -207,7 +209,7 @@
             ext[2, field, x + 1] = jnp.where(is_last, right, ext[2, field, x + 1])
         return 0
 
-    lax.fori_loop(0, LX, fix_body, 0, unroll=8)
+    lax.fori_loop(0, LX, fix_body, 0, unroll=16)
     for row, rows, slot, at in ((0, xlo, 0, LX - 1), (LX + 1, xhi, 2, 0)):
         for field in range(4):
             spot = field * LX + at
@@ -259,7 +261,7 @@
         ay_k[pl.ds(x, K, stride=LX), :] = totals[3]
         return 0
 
-    lax.fori_loop(0, LX, advect_body, 0)
+    lax.fori_loop(0, LX, advect_body, 0, unroll=2)
     block = LX * K
     stores = [
         pltpu.make_async_copy(o_dens, o_dens_hbm, io_sem.at[12]),
@@ -282,7 +284,7 @@
                 descriptor(simp(balanced(i, S)), me).start()
                 return 0
 
-            lax.fori_loop(first, end, body, 0)
+            lax.fori_loop(first, end, body, 0, unroll=4)
 
         def wait_recv():
             def body(off, _):

time: 79.1 us -> 78.1 us (0.987)
  Pallas kernels: 78.2 us -> 77 us
    pallas_call x1, Pallas kernels: 75.2 us -> 74 us  [shards(): pl.pallas_call(functools.partial(step_kernel, (S, N, LX, K, VIEWS)), out_...]
where the time goes in v5:
time: 78.1 us; the launch traced here: 77.6 us
  Pallas kernels  77 us (99%)
    pallas_call x1, Pallas kernels, shards(): pl.pallas_call(functools.partial(step_kernel, (S, N, LX, K, VIEWS)), out_...  74 us
    pallas_call x1, Pallas kernels, shards(): pl.pallas_call(hand_over, out_shape=shapes, in_specs=[anywhere] * 4, out_...  3 us

profile of v5, /device:TPU:1, one launch (start us, length us, event | category | flops | bytes accessed | tf_op | source)
XLA Modules:
  0.0 77.6 jit_solution(12586778576102654276)
XLA Ops:
  0.6 74.0 %shard_map.129 = (f32[1024,128]{1,0:T(8,128)}, f32[3072,128]{1,0:T(8,128)}, f32[32,1,128]{2,1,0:T(1,128)}, f32[1024,128]{1,0:T(8,128)}) custom-call(f32[32,32,128]{2,1,0:T(8,128)} %dens_hbm.1, f32[3,32,32,128]{3,2,1,0:T(8,128)} %vel_hbm.1, s32[32,32,128]{2,1,0:T(8,128)} %code_hbm.1, f32[3,32,32,128]{3,2,1,0:T(8,128)} %frac_hbm.1, f32[32,1,128]{2,1,0:T(1,128)} %targ.1, ...), custom_call_target="tpu_custom_call" | custom-call | tf_op jit(solution)/shard_map/pallas_call | solution.py:846
  74.6 3.0 %shard_map.130 = (f32[1024,128]{1,0:T(8,128)}, f32[3072,128]{1,0:T(8,128)}, f32[32,1,128]{2,1,0:T(1,128)}, f32[1024,128]{1,0:T(8,128)}) custom-call(f32[1024,128]{1,0:T(8,128)} %get-tuple-element.12.refs_0_, f32[3072,128]{1,0:T(8,128)} %get-tuple-element.13.refs_1_, f32[32,1,128]{2,1,0:T(1,128)} %get-tuple-element.14.refs_2_, ...), custom_call_target="tpu_custom_call" | custom-call | tf_op jit(solution)/shard_map/pallas_call | solution.py:863
